TPU v7x, 128 devices: a whole 4x4x4 slice. The times are simulated.
128 devices in a mesh: rep: 16 (over x_lo, y, core), shard: 8 (over z, x_hi).
Axes of the slice: x: 4 (x_hi: 2, x_lo: 2; x = x_hi * 2 + x_lo), y: 4, z: 4, core: 2. Of those that a mesh axis runs over, the one named last changes fastest.
Arguments:
- block_input: bfloat16 [16, 1024, 1024], P('rep', 'shard'), may hold values from -6 to 6
- attn_gain: bfloat16 [1024], P('shard'), may hold values from 0.5 to 1.5
- attn_bias: bfloat16 [1024], P('shard'), may hold values from -4 to 4
- query_key_value_weight: bfloat16 [1024, 3072], P('shard'), may hold values from -0.1875 to 0.1875
- query_key_value_bias: bfloat16 [3072], P('shard'), may hold values from -6 to 6
- output_projection_weight: bfloat16 [1024, 1024], P('shard'), may hold values from -0.75 to 0.75
- mlp_gain: bfloat16 [1024], P('shard'), may hold values from 0.5 to 1.5
- mlp_bias: bfloat16 [1024], P('shard'), may hold values from -4 to 4
- gate_up_projection_weight: bfloat16 [1024, 5632], P('shard'), may hold values from -0.1875 to 0.1875
- down_projection_weight: bfloat16 [2816, 1024], P('shard'), may hold values from -0.109375 to 0.109375
- out_grad: bfloat16 [16, 1024, 1024], P('rep', 'shard'), may hold values from -6 to 6
Outputs:
- block_output: bfloat16 [16, 1024, 1024], P('rep', 'shard')
- input_grad: bfloat16 [16, 1024, 1024], P('rep', 'shard')
- attn_gain_grad: float32 [1024], P('shard')
- attn_bias_grad: float32 [1024], P('shard')
- qkv_weight_grad: float32 [1024, 3072], P('shard')
- qkv_bias_grad: float32 [3072], P('shard')
- out_weight_grad: float32 [1024, 1024], P('shard')
- mlp_gain_grad: float32 [1024], P('shard')
- mlp_bias_grad: float32 [1024], P('shard')
- gate_up_weight_grad: float32 [1024, 5632], P('shard')
- down_weight_grad: float32 [2816, 1024], P('shard')
All inputs are finite; a program needn't handle non-finite values.
Results may differ from a plain program's by a relative error of at most 0.025.
Values may be sent and summed in bfloat16 or wider, within the bound.
No kernel may reach another device: no remote copies, remote signals or barrier semaphores. Data moves between devices by JAX's collectives and lax.ppermute only.
A program may use at most 128 MiB of HBM per device.

v0:
```python
import jax
import jax.numpy as jnp
import numpy as np
from jax import lax
from jax.experimental import pallas as pl
from jax.experimental.pallas import tpu as pltpu
from jax.sharding import PartitionSpec as P

D = 1024
HEADS = 16
HEAD_DIM = 64
FF = 2816
ROTARY = 16
SEQ = 1024
BLOCK = 256
UNITS = 352
PAD = 384

EPSILON = 1e-05
SCORE_SCALE = 0.125

SHARD = ("z", "xh")
PLANE = ("xl", "y")
F32 = jnp.float32
BF16 = jnp.bfloat16
MIB = 1024 * 1024

VEC_AT, QKV_AT, GU_AT = 1024, 1040, 1232


def normalize(values):
    center = values - jnp.mean(values, axis=-1, keepdims=True)
    variance = jnp.mean(center * center, axis=-1, keepdims=True)
    inverse = lax.rsqrt(variance + EPSILON)
    return (center * inverse, inverse)


def norm_back(scaled_grad, normed, inverse):
    return inverse * (
        scaled_grad
        - jnp.mean(scaled_grad, axis=-1, keepdims=True)
        - normed * jnp.mean(scaled_grad * normed, axis=-1, keepdims=True)
    )


def rotary_tables():
    half = ROTARY // 2
    frequency = np.float32(10000.0) ** (-np.arange(half, dtype=np.float32) * np.float32(2.0) / np.float32(ROTARY))
    angles = np.arange(SEQ, dtype=np.float32)[None, :] * frequency.astype(np.float32)[:, None]
    return np.cos(angles).astype(np.float32), np.sin(angles).astype(np.float32)


def exchange(value, axes):
    return lax.all_to_all(value, axes, 0, 0, tiled=True)


def spread(value, axes, count):
    return exchange(jnp.broadcast_to(value[None], (count,) + value.shape), axes)


def swap(value, axis):
    return lax.ppermute(value, axis, [(0, 1), (1, 0)])


def turn(value, axis, step):
    return lax.ppermute(value, axis, [(i, (i + step) % 4) for i in range(4)])


def index_of(xl, y, c, z, xh):
    return (((xl * 4 + y) * 2 + c) * 4 + z) * 2 + xh


def move(value, target):
    pairs = []
    for xl in range(2):
        for y in range(4):
            for c in range(2):
                for z in range(4):
                    for xh in range(2):
                        pairs.append((index_of(xl, y, c, z, xh), index_of(*target(xl, y, c, z, xh))))
    return lax.ppermute(value, ("xl", "y", "c", "z", "xh"), pairs)


def tie(*values):
    return lax.optimization_barrier(values)


def dot(a, b, dims=((1,), (0,))):
    return lax.dot_general(a, b, (dims, ((), ())), preferred_element_type=F32)


NT = ((1,), (1,))

ID_Y, ID_C, ID_Z, ID_XH, ID_XL = range(5)


class Part:
    def __init__(self, array, count, dims, views):
        self.array, self.shape, self.dtype, self.views = array, (count,) + dims, array.dtype, views


class Later:
    def __init__(self, copies, buffer):
        self.copies, self.buffer = copies, buffer

    def arrive(self):
        for copy in self.copies:
            copy.wait()
        self.copies = []
        return self.buffer

    def __getitem__(self, index):
        return self.arrive()[index]


class Result:
    def __init__(self, copy, buffer):
        self.copy, self.buffer, self.sent = copy, buffer, False

    def __setitem__(self, index, value):
        self.buffer[index] = value

    def __getitem__(self, index):
        return self.buffer[index]

    def send(self):
        if not self.sent:
            self.copy.start()
            self.sent = True


def call(kernel, name, out_shape, args, scratch=(), moved=1):
    count, outs, own = len(args) - 1, len(out_shape), len(scratch)

    def body(ids, *refs):
        sources, rest = refs[:count], refs[count:]
        targets, mine, rest = rest[:outs], rest[outs : outs + own], rest[outs + own :]
        buffers, results, (sems, out_sems) = rest[:count], rest[count:-2], rest[-2:]
        inputs = []
        at = 0
        for i in range(count):
            if isinstance(args[i + 1], Part):
                views = args[i + 1].views(sources[i], ids)
                copies = [
                    pltpu.make_async_copy(view, buffers[i].at[j], sems.at[at + j]) for j, view in enumerate(views)
                ]
            else:
                copies = [pltpu.make_async_copy(sources[i], buffers[i], sems.at[at])]
            at += len(copies)
            for copy in copies:
                copy.start()
            inputs.append(Later(copies, buffers[i]))
        outputs = [
            Result(pltpu.make_async_copy(results[i], targets[i], out_sems.at[i]), results[i]) for i in range(outs)
        ]
        kernel(ids, *inputs, *outputs, *mine)
        for value in inputs:
            value.arrive()
        for value in outputs:
            value.send()
        for value in outputs:
            value.copy.wait()

    flights = sum(a.shape[0] if isinstance(a, Part) else 1 for a in args[1:])
    return pl.pallas_call(
        body,
        out_shape=out_shape,
        in_specs=[pl.BlockSpec(memory_space=pltpu.SMEM)] + [pl.BlockSpec(memory_space=pltpu.HBM)] * count,
        out_specs=tuple(pl.BlockSpec(memory_space=pltpu.HBM) for _ in out_shape),
        scratch_shapes=list(scratch)
        + [pltpu.VMEM(a.shape, a.dtype) for a in list(args[1:]) + list(out_shape)]
        + [pltpu.SemaphoreType.DMA((flights,)), pltpu.SemaphoreType.DMA((outs,))],
        compiler_params=pltpu.CompilerParams(vmem_limit_bytes=60 * MIB),
        cost_estimate=pl.CostEstimate(flops=0, bytes_accessed=moved, transcendentals=0),
        name=name,
    )(*[a.array if isinstance(a, Part) else a for a in args])


def shape(*dims, dtype=BF16):
    return jax.ShapeDtypeStruct(dims, dtype)


def turned(value, cos, sin, sign):
    a = value[0:8]
    b = value[8:16]
    return jnp.concatenate([a * cos - sign * (b * sin), b * cos + sign * (a * sin), value[16:]], axis=0)


def qkv_weights(c, packet, other, w_rows, w_out):
    mine = pl.multiple_of(c * 64, 64)
    theirs = pl.multiple_of((1 - c) * 64, 64)
    for src in range(8):
        for kind in range(3):
            lanes = slice(kind * 128, kind * 128 + 128)
            at = QKV_AT + kind * 64
            w_rows[pl.ds(src * 128 + mine, 64), lanes] = packet[0, src, at : at + 64, :]
            w_rows[pl.ds(src * 128 + theirs, 64), lanes] = other[src, kind * 64 : kind * 64 + 64, :]
    for kind in range(3):
        for src in range(8):
            w_out[kind * 128 : kind * 128 + 128, src * 128 : src * 128 + 128] = w_rows[
                src * 128 : src * 128 + 128, kind * 128 : kind * 128 + 128
            ].T


def normed_kernel(ids, packet, xhat_out):
    for block in range(8):
        x = jnp.concatenate([packet[0, block, cb * 128 : cb * 128 + 128, :].astype(F32) for cb in range(8)], axis=1)
        xhat_out[block * 128 : block * 128 + 128, :] = normalize(x)[0].astype(BF16)


def attend_kernel(ids, packet, other, cos_ref, sin_ref, qkv_out, attended, lse_out, w_out, w_rows):
    c = ids[ID_C]
    s = ids[ID_Z] * 2 + ids[ID_XH]
    qkv_weights(c, packet, other, w_rows, w_out)
    w_out.send()
    vec = [packet[0, src, VEC_AT : VEC_AT + 16, :].astype(F32) for src in range(8)]
    gain = jnp.concatenate([v[0:1] for v in vec], axis=1)
    bias = jnp.concatenate([v[1:2] for v in vec], axis=1)
    row = lax.broadcasted_iota(jnp.int32, (16, 128), 0)
    qkv_bias = []
    for kind in range(3):
        total = jnp.zeros((16, 128), F32)
        for src in range(8):
            total += jnp.where((row >= 4) & (row < 7) & (row - 4 + 3 * src == 8 * kind + s), vec[src], 0.0)
        line = jnp.sum(total, axis=0, keepdims=True)
        qkv_bias.append(jnp.broadcast_to(line, (128, 128)).T)
    qkv_bias = jnp.concatenate(qkv_bias, axis=0)
    qkv_bias = jnp.concatenate([qkv_bias, qkv_bias], axis=1)
    for block in range(SEQ // BLOCK):
        lo = block * BLOCK
        x = jnp.concatenate(
            [
                jnp.concatenate(
                    [packet[0, 2 * block + i, cb * 128 : cb * 128 + 128, :].astype(F32) for cb in range(8)], axis=1
                )
                for i in range(2)
            ],
            axis=0,
        )
        normed, _ = normalize(x)
        first_in = (normed * gain + bias).astype(BF16)
        part = dot(w_out[...], first_in, NT) + qkv_bias
        cos = cos_ref[:, lo : lo + BLOCK]
        sin = sin_ref[:, lo : lo + BLOCK]
        for kind in range(3):
            for head in range(2):
                base = kind * 128 + head * 64
                full = part[base : base + 64]
                if kind < 2:
                    full = turned(full, cos, sin, 1.0)
                qkv_out[base : base + 64, lo : lo + BLOCK] = full.astype(BF16)
    qkv_out.send()
    row = lax.broadcasted_iota(jnp.int32, (BLOCK, BLOCK), 0)
    col = lax.broadcasted_iota(jnp.int32, (BLOCK, BLOCK), 1)
    lse_out[...] = jnp.zeros((8, SEQ), F32)
    for block in range(SEQ // BLOCK):
        lo = block * BLOCK
        hi = lo + BLOCK
        both = []
        for head in range(2):
            keys = qkv_out[128 + head * 64 : 128 + head * 64 + 64, :hi].T
            value_t = qkv_out[256 + head * 64 : 256 + head * 64 + 64, :hi]
            query_t = qkv_out[head * 64 : head * 64 + 64, lo:hi] * jnp.bfloat16(SCORE_SCALE)
            parts = []
            if block:
                parts.append(dot(keys[:lo], query_t))
            parts.append(jnp.where(row <= col, dot(keys[lo:hi], query_t), -jnp.inf))
            scores = jnp.concatenate(parts, axis=0) if block else parts[0]
            top = jnp.max(scores, axis=0, keepdims=True)
            exps = jnp.exp(scores - top)
            total = jnp.sum(exps, axis=0, keepdims=True)
            both.append(dot(value_t, exps.astype(BF16)) / total)
            lse_out[head : head + 1, lo:hi] = top + jnp.log(total)
        out = jnp.concatenate(both, axis=0).T.astype(BF16)
        for parity in range(2):
            for zt in range(4):
                attended[2 * zt + parity, block * 128 : block * 128 + 128, :] = out[parity * 128 : parity * 128 + 128]


def weights_kernel(ids, p0, p1, p2, p3, p4, p5, p6, p7, gate_w, up_w, out_w):
    y, c = ids[ID_Y], ids[ID_C]
    for k, refs in enumerate(((p0, p4), (p1, p5), (p2, p6), (p3, p7))):
        at = pl.multiple_of(lax.rem(y - k + 4, 4) * 32, 32)
        for core, ref in enumerate(refs):
            half = c if core == 0 else 1 - c
            for src in range(8):
                rows = pl.ds(src * 128 + at, 32)
                for cb in range(3):
                    lanes = slice(core * PAD + cb * 128, core * PAD + cb * 128 + 128)
                    gate_w[rows, lanes] = ref[src, cb * 32 : cb * 32 + 32, :]
                    up_w[rows, lanes] = ref[src, 96 + cb * 32 : 96 + cb * 32 + 32, :]
                for cb in range(4):
                    lanes = pl.ds(pl.multiple_of(half * 512 + cb * 128, 128), 128)
                    out_w[rows, lanes] = ref[src, 192 + cb * 32 : 192 + cb * 32 + 32, :]


def assemble_down(ids, own, other, down_w):
    swapped = jnp.where(ids[ID_XH] == ids[ID_C], 0, PAD)
    down_w[pl.ds(pl.multiple_of(swapped, 128), UNITS), :] = own[...]
    down_w[pl.ds(pl.multiple_of(PAD - swapped, 128), UNITS), :] = other[...]
    for base in (UNITS, PAD + UNITS):
        down_w[base : base + PAD - UNITS, :] = jnp.zeros((PAD - UNITS, D), BF16)


def cotangent(parts):
    return jnp.concatenate([part[...] for part in parts], axis=0)


def mlp_kernel(
    ids, out_w, att, x_ref, gate_w, up_w, gain_ref, bias_ref, dy0, dy1, dy2, dy3, down_own, down_other, mixed_own, att_out, small, ds, keep, send, out0, out1, out2, out3, down_w, second_out, hidden_out, dgate_out, dup_out, held
):
    z = ids[ID_Z]
    gain = gain_ref[...]
    bias = bias_ref[...]
    gain_sum = jnp.zeros((1, D), F32)
    bias_sum = jnp.zeros((1, D), F32)
    for pair in range(2):
        rows = slice(pair * 256, pair * 256 + 256)
        a_parts = []
        x_parts = []
        for k in (2 * pair, 2 * pair + 1):
            place = lax.rem(z - k + 4, 4)
            at = pl.ds(pl.multiple_of(place * 128, 128), 128)
            a_parts.append(jnp.concatenate([att[src, at, :] for src in range(8)], axis=1))
            x_parts.append(
                jnp.concatenate([x_ref[k, cb * 128 : cb * 128 + 128, :] for cb in range(8)], axis=1)
            )
        attended = jnp.concatenate(a_parts, axis=0)
        att_out[rows, :] = attended
        mixed = jnp.concatenate(x_parts, axis=0).astype(F32) + dot(attended, out_w[...])
        if pair == 0:
            mixed_own[...] = mixed[:128]
        normed, _ = normalize(mixed)
        second_in = (normed * gain + bias).astype(BF16)
        second_out[rows, :] = second_in
        gate = dot(second_in, gate_w[...])
        up_part = dot(second_in, up_w[...])
        sig = jax.nn.sigmoid(gate)
        silu = gate * sig
        hidden_out[rows, :] = (silu * up_part).astype(BF16)
        dy = cotangent((dy0, dy1, dy2, dy3)[2 * pair : 2 * pair + 2])
        if pair == 0:
            assemble_down(ids, down_own, down_other, down_w)
        dhidden = dot(dy, down_w[...], NT)
        dgate = (dhidden * up_part * sig * (1.0 + gate * (1.0 - sig))).astype(BF16)
        dup = (dhidden * silu).astype(BF16)
        dgate_out[rows, :] = dgate
        dup_out[rows, :] = dup
        dsecond = dot(dgate, gate_w[...], NT) + dot(dup, up_w[...], NT)
        gain_sum += jnp.sum(dsecond * normed, axis=0, keepdims=True)
        bias_sum += jnp.sum(dsecond, axis=0, keepdims=True)
        low = dsecond.astype(BF16)
        for i in range(2):
            ds[lax.rem(z - (2 * pair + i) + 4, 4)] = low[i * 128 : i * 128 + 128]
    small[...] = jnp.concatenate([gain_sum, bias_sum, jnp.zeros((6, D), F32)], axis=0)
    ds.send()
    att_out.send()

    y, c, xh, xl = ids[ID_Y], ids[ID_C], ids[ID_XH], ids[ID_XL]

    def place(to_y):
        return lax.rem(y - to_y + 4, 4)

    for block in range(4):
        turned_in = second_out[:, block * 256 : block * 256 + 256].T
        for which, grad in ((0, dgate_out), (1, dup_out)):
            part = dot(turned_in, grad[...]).astype(BF16)
            for target, base in ((keep, 0), (send, PAD)):
                for i in range(16):
                    owner, to_xl, to_y = block * 2 + i // 8, (i // 4) % 2, i % 4
                    for cb in range(3):
                        at = (owner * 2 + to_xl) * 96 + (which * 3 + cb) * 16
                        target[place(to_y), at : at + 16, :] = part[
                            i * 16 : i * 16 + 16, base + cb * 128 : base + cb * 128 + 128
                        ]
    hidden_t = hidden_out[...].T
    held[...] = dot(hidden_t, cotangent((dy0, dy1, dy2, dy3))).astype(BF16)
    for target, half in ((keep, c), (send, 1 - c)):
        for base, to_xh in ((0, c), (PAD, 1 - c)):
            for to_xl in range(2):
                rows = pl.ds(pl.multiple_of(1536 + jnp.abs(xh - to_xh) * 352 + to_xl * 176, 16), 176)
                for cb in range(4):
                    lanes = pl.ds(pl.multiple_of(half * 512 + cb * 128, 128), 128)
                    target[place(cb), rows, :] = held[base + to_xl * 176 : base + to_xl * 176 + 176, lanes]
    send.send()
    keep.send()
    for pair in range(2):
        part = dot(hidden_out[pair * 256 : pair * 256 + 256, :], down_w[...]).astype(BF16)
        ((out0, out1), (out2, out3))[pair][0][...] = part[:128]
        ((out0, out1), (out2, out3))[pair][1][...] = part[128:]


def norm_kernel(ids, ds, dy, mixed_ref, gain_ref, out_w, dmixed_out, blocks):
    dsecond = ds[0].astype(F32) + ds[1].astype(F32) + ds[2].astype(F32) + ds[3].astype(F32)
    normed, inverse = normalize(mixed_ref[...])
    dmixed = dy[...].astype(F32) + norm_back(dsecond * gain_ref[...], normed, inverse)
    dmixed_out[...] = dmixed
    dproj = dmixed.astype(BF16)
    dattended = dot(dproj, out_w[...], NT).astype(BF16)
    for dest in range(8):
        blocks[dest, :128, :] = dattended[:, dest * 128 : dest * 128 + 128]
        for cb in range(2):
            at = (dest // 2) * 256 + cb * 128
            blocks[dest, 128 + cb * 128 : 256 + cb * 128, :] = dproj[:, at : at + 128]


def attend_back_kernel(
    ids, blocks, qkv, lse_ref, cos_ref, sin_ref, xhat, w_t, gain_ref, bias_ref, small, att, keep, send, dq_keep,
    dq_send, dkey, dvalue, dq_t, dq_rows, grad_rows, out_rows
):
    c, z, xh = ids[ID_C], ids[ID_Z], ids[ID_XH]
    cos = cos_ref[...]
    sin = sin_ref[...]
    row = lax.broadcasted_iota(jnp.int32, (BLOCK, BLOCK), 0)
    col = lax.broadcasted_iota(jnp.int32, (BLOCK, BLOCK), 1)
    for head in range(2):
        dkey[...] = jnp.zeros_like(dkey)
        dvalue[...] = jnp.zeros_like(dvalue)
        key_t = qkv[128 + head * 64 : 128 + head * 64 + 64, :]
        keys = key_t.T
        values = qkv[256 + head * 64 : 256 + head * 64 + 64, :].T
        dquery = []
        for block in range(SEQ // BLOCK):
            lo = block * BLOCK
            hi = lo + BLOCK
            query_t = qkv[head * 64 : head * 64 + 64, lo:hi] * jnp.bfloat16(SCORE_SCALE)
            query = query_t.T
            grad = jnp.concatenate(
                [blocks[2 * block + i, :128, head * 64 : head * 64 + 64] for i in range(2)], axis=0
            )
            grad_t = grad.T
            lse = lse_ref[head : head + 1, lo:hi]
            parts = []
            if block:
                parts.append(jnp.exp(dot(keys[:lo], query_t) - lse))
            parts.append(jnp.where(row <= col, jnp.exp(dot(keys[lo:hi], query_t) - lse), 0.0))
            shares = jnp.concatenate(parts, axis=0) if block else parts[0]
            dshares = dot(values[:hi], grad_t)
            row_dot = jnp.sum(shares * dshares, axis=0, keepdims=True)
            dscores = (shares * (dshares - row_dot)).astype(BF16)
            dvalue[:hi] += dot(shares.astype(BF16), grad)
            dkey[:hi] += dot(dscores, query)
            dquery.append(dot(key_t[:, :hi], dscores) * SCORE_SCALE)
        dquery_t = jnp.concatenate(dquery, axis=1)
        dq_t[head * 64 : head * 64 + 64, :] = turned(dquery_t, cos, sin, -1.0).astype(BF16)
        dq_t[128 + head * 64 : 128 + head * 64 + 64, :] = turned(dkey[...].T, cos, sin, -1.0).astype(BF16)
        dq_t[256 + head * 64 : 256 + head * 64 + 64, :] = dvalue[...].T.astype(BF16)
    whole = dq_t[...]
    sums = jnp.sum(whole.astype(F32), axis=1, keepdims=True)
    product = dot(whole, xhat[...])
    weights = w_t[...].astype(F32)
    gain_part = jnp.sum(product * weights, axis=0, keepdims=True)
    bias_part = jnp.sum(sums * weights, axis=0, keepdims=True)
    grad_rows[...] = (product * gain_ref[...] + sums * bias_ref[...]).T
    dproj = jnp.concatenate(
        [
            jnp.concatenate(
                [blocks[2 * lax.rem(z - k + 4, 4) + xh, 128 + cb * 128 : 256 + cb * 128, :] for cb in range(2)], axis=1
            )
            for k in range(4)
        ],
        axis=0,
    )
    for block in range(4):
        rows = slice(block * 256, block * 256 + 256)
        out_rows[rows, :] = dot(att[:, rows].T, dproj)
    lines = [
        jnp.broadcast_to(sums[kind * 128 : kind * 128 + 128], (128, 128)).T[0:1] for kind in range(3)
    ]
    filler = jnp.zeros((7, 128), F32)
    for dest in range(8):
        lanes = slice(dest * 128, dest * 128 + 128)
        lines_here = [gain_part[:, lanes], bias_part[:, lanes], small[0:1, lanes], small[1:2, lanes]] + lines
        lines_here.append(jnp.zeros((1, 128), F32))
        for e in range(8):
            tail = jnp.concatenate([lines_here[e], filler], axis=0)
            for target, half in ((keep, c), (send, 1 - c)):
                rows = pl.ds(pl.multiple_of(dest * 128 + half * 64 + e * 8, 8), 8)
                target[dest * 8 + e] = jnp.concatenate(
                    [grad_rows[rows, kind * 128 : kind * 128 + 128] for kind in range(3)]
                    + [out_rows[rows, cb * 128 : cb * 128 + 128] for cb in range(2)]
                    + [tail],
                    axis=0,
                ).astype(BF16)
    keep.send()
    send.send()
    dq_rows[...] = whole.T
    for k in range(4):
        base = lax.rem(z - k + 4, 4) * 256
        dq_keep[k * 128 : k * 128 + 128, :] = dq_rows[pl.ds(pl.multiple_of(base + xh * 128, 128), 128), :]
        theirs = pl.ds(pl.multiple_of(base + (1 - xh) * 128, 128), 128)
        for kind in range(3):
            at = kind * 512 + k * 128
            dq_send[at : at + 128, :] = dq_rows[theirs, kind * 128 : kind * 128 + 128]


def mlp_grad_kernel(ids, m0, m1, m2, m3, o0, o1, o2, o3, gate_up, down):
    c, y, xl = ids[ID_C], ids[ID_Y], ids[ID_XL]
    mine, other = (m0, m1, m2, m3), (o0, o1, o2, o3)
    zero = c == 0

    def place(k, i):
        return lax.rem(xl + i, 2), lax.rem(y - k + 4, 4)

    def wide(ref, i, z, which):
        at = z * 96 + which * 48
        return jnp.concatenate(
            [ref[i, at + cb * 16 : at + cb * 16 + 16, :].astype(F32) for cb in range(3)], axis=1
        )[:, :UNITS]

    for k in range(4):
        for i in range(2):
            to_xl, to_y = place(k, i)
            rows = pl.ds(pl.multiple_of(to_xl * 64 + to_y * 16, 16), 16)
            for which in range(2):
                parts = []
                for z in range(4):
                    a, b = wide(mine[k], i, z, which), wide(other[k], i, z, which)
                    parts += [jnp.where(zero, a, b), jnp.where(zero, b, a)]
                gate_up[rows, which * FF : which * FF + FF] = jnp.concatenate(parts, axis=1)
    gate_up.send()
    for refs, half in ((mine, c), (other, 1 - c)):
        for k in range(4):
            lanes = pl.ds(pl.multiple_of(half * 512 + place(k, 0)[1] * 128, 128), 128)
            down[:, lanes] = refs[k][0, 384:736, :].astype(F32) + refs[k][1, 384:736, :].astype(F32)


def qkv_grad_kernel(ids, mine, other, qkv, out_w, qkv_bias, attn_gain, attn_bias, mlp_gain, mlp_bias):
    c = ids[ID_C]
    s = ids[ID_Z] * 2 + ids[ID_XH]
    totals = []
    for ref, half in ((mine, c), (other, 1 - c)):
        for e in range(8):
            rows = pl.ds(pl.multiple_of(half * 64 + e * 8, 8), 8)
            tiles = [ref[e, src * 48 : src * 48 + 48, :].astype(F32) for src in range(8)]
            for src in range(8):
                for kind in range(3):
                    lanes = slice(kind * D + src * 128, kind * D + src * 128 + 128)
                    qkv[rows, lanes] = tiles[src][kind * 8 : kind * 8 + 8]
            for z in range(4):
                for cb in range(2):
                    lanes = slice(z * 256 + cb * 128, z * 256 + cb * 128 + 128)
                    at = slice(24 + cb * 8, 32 + cb * 8)
                    out_w[rows, lanes] = tiles[2 * z][at] + tiles[2 * z + 1][at]
            if ref is mine:
                totals.append([tile[40:41] for tile in tiles])
    for e, vector in enumerate((attn_gain, attn_bias, mlp_gain, mlp_bias)):
        total = totals[e][0]
        for line in totals[e][1:]:
            total = total + line
        vector[...] = total
    for i in range(3):
        block = 3 * s + i
        found = jnp.zeros((1, 128), F32)
        for src in range(8):
            for kind in range(3):
                found += jnp.where(block == 8 * kind + src, totals[4 + kind][src], 0.0)
        qkv_bias[:, i * 128 : i * 128 + 128] = found


def shards(
    block_input,
    attn_gain,
    attn_bias,
    query_key_value_weight,
    query_key_value_bias,
    output_projection_weight,
    mlp_gain,
    mlp_bias,
    gate_up_projection_weight,
    down_projection_weight,
    out_grad,
):
    y = lax.axis_index("y")
    c = lax.axis_index("c")
    z = lax.axis_index("z")
    xh = lax.axis_index("xh")
    xl = lax.axis_index("xl")
    ids = jnp.stack([y, c, z, xh, xl]).astype(jnp.int32)
    x_own = block_input[0]
    dy_own = out_grad[0]
    cos_np, sin_np = rotary_tables()
    cos, sin = jnp.asarray(cos_np), jnp.asarray(sin_np)

    gu_rows = lax.dynamic_slice_in_dim(gate_up_projection_weight, y * 32, 32, 0).reshape(32, 2, 4, 2, UNITS)
    gu_rows = lax.dynamic_index_in_dim(gu_rows, c, 3, keepdims=False)
    gu_rows = jnp.pad(gu_rows, ((0, 0), (0, 0), (0, 0), (0, PAD - UNITS))).reshape(32, 2, 4, 3, 128)
    gu_part = jnp.broadcast_to(gu_rows.transpose(2, 1, 3, 0, 4).reshape(4, 1, 192, 128), (4, 2, 192, 128))
    out_rows = lax.dynamic_slice(output_projection_weight, (y * 32, c * 512), (32, 512))
    out_part = out_rows.reshape(32, 4, 128).transpose(1, 0, 2).reshape(128, 128)
    tail = jnp.broadcast_to(out_part[None], (8, 128, 128))

    x_part = x_own.reshape(128, 8, 128).transpose(1, 0, 2).reshape(D, 128)
    vec = jnp.concatenate(
        [
            jnp.stack([attn_gain, attn_bias, mlp_gain, mlp_bias]),
            query_key_value_bias.reshape(3, 128),
            jnp.zeros((9, 128), BF16),
        ]
    )
    qkv_rows = lax.dynamic_slice_in_dim(query_key_value_weight, c * 64, 64, 0)
    qkv_part = qkv_rows.reshape(64, 3, 8, 128).transpose(2, 1, 0, 3).reshape(8, 192, 128)
    head = jnp.broadcast_to(jnp.concatenate([x_part, vec])[None], (8, QKV_AT, 128))
    packet = jnp.concatenate([head, qkv_part, gu_part.reshape(8, 192, 128), tail], axis=1)
    packet, down_now = tie(exchange(packet, SHARD), down_projection_weight)
    down_other = swap(down_now, "xh")
    piece = packet[:, GU_AT:]
    before, after = turn(piece, "y", 1), turn(piece, "y", 3)
    qkv_other = swap(packet[:, QKV_AT:GU_AT], "c")
    head_of = lambda array: Part(array, 1, (8, GU_AT, 128), lambda ref, ids: [ref.at[:, 0:GU_AT]])
    qkv_t, att_blocks, lse, w_t = call(
        attend_kernel,
        "attend_forward",
        (shape(384, SEQ), shape(8, 512, 128), shape(8, SEQ, dtype=F32), shape(384, D)),
        (ids, head_of(packet), qkv_other, cos, sin),
        scratch=[pltpu.VMEM((D, 384), BF16)],
    )
    att_blocks, packet_late, far, dy_now = tie(att_blocks, packet, piece, dy_own)
    pieces = [piece, before, turn(far, "y", 2), after]
    dys = [dy_now] + [turn(dy_now, "z", k) for k in (1, 2, 3)]
    att = exchange(att_blocks, SHARD)
    (xhat,) = call(
        normed_kernel,
        "normed_input",
        (shape(SEQ, D),),
        (ids, Part(packet_late, 1, (8, D, 128), lambda ref, ids: [ref.at[:, 0:D]])),
    )
    pieces += [swap(p, "c") for p in pieces]
    gate_w, up_w, out_w = call(
        weights_kernel,
        "weights",
        (shape(D, 2 * PAD), shape(D, 2 * PAD), shape(D, D)),
        (ids, *pieces),
    )

    vecs = packet[:, VEC_AT : VEC_AT + 4].astype(F32).transpose(1, 0, 2).reshape(4, 1, D)
    gain_one, bias_one, gain_two, bias_two = vecs[0], vecs[1], vecs[2], vecs[3]
    out_w, xhat = tie(out_w, xhat)
    w_t_other = swap(w_t, "xh")

    mixed_own, att_rel, mlp_small, ds, keep, send, *outs = call(
        mlp_kernel,
        "mlp",
        (
            shape(128, D, dtype=F32),
            shape(512, D),
            shape(8, D, dtype=F32),
            shape(4, 128, D),
            shape(4, 2240, 128),
            shape(4, 2240, 128),
        )
        + (shape(128, D),) * 4,
        (
            ids,
            out_w,
            att,
            Part(
                packet,
                4,
                (D, 128),
                lambda ref, ids: [ref.at[2 * lax.rem(ids[ID_Z] - k + 4, 4) + ids[ID_XH], 0:D] for k in range(4)],
            ),
            gate_w,
            up_w,
            gain_two,
            bias_two,
            *dys,
            down_projection_weight,
            down_other,
        ),
        scratch=[pltpu.VMEM((2 * PAD, D), BF16), pltpu.VMEM((512, D), BF16)]
        + [pltpu.VMEM((512, 2 * PAD), BF16)] * 3
        + [pltpu.VMEM((2 * PAD, D), BF16)],
    )
    ds = exchange(ds, "z")
    mlp_chunks = (keep.astype(F32) + swap(send, "c").astype(F32)).astype(BF16)
    dmixed, blocks = call(
        norm_kernel,
        "norm_backward",
        (shape(128, D, dtype=F32), shape(8, 384, 128)),
        (ids, ds, dy_own, mixed_own, gain_two, out_w),
    )
    blocks = exchange(blocks, SHARD)

    mlp_y = mlp_chunks[0].astype(F32)
    for k in (1, 2, 3):
        mlp_y = mlp_y + turn(mlp_chunks[k], "y", -k).astype(F32)
    mlp_y = mlp_y.astype(BF16)

    grad_keep, grad_send, dq_keep, dq_send = call(
        attend_back_kernel,
        "attend_backward",
        (shape(64, 48, 128), shape(64, 48, 128), shape(512, 384), shape(1536, 128)),
        (ids, blocks, qkv_t, lse, cos, sin, xhat, w_t, gain_one, bias_one, mlp_small, att_rel),
        scratch=[
            pltpu.VMEM((SEQ, HEAD_DIM), F32),
            pltpu.VMEM((SEQ, HEAD_DIM), F32),
            pltpu.VMEM((384, SEQ), BF16),
            pltpu.VMEM((SEQ, 384), BF16),
            pltpu.VMEM((D, 384), F32),
            pltpu.VMEM((D, 256), F32),
        ],
    )

    gu_recv = exchange(mlp_y[:1536].reshape(16, 96, 128), ("z", "xh", "xl"))
    grad_send, gu_recv, w_t_other = tie(grad_send, gu_recv, w_t_other)
    chunks = (grad_keep.astype(F32) + swap(grad_send, "c").astype(F32)).astype(BF16)
    chunks, dq_send = tie(chunks, dq_send)
    both = swap(jnp.concatenate([dq_send, mlp_y[1888:2240]], axis=0), "xh")
    dq_recv = both[:1536].reshape(3, 512, 128)
    do_piece = (mlp_y[1536:1888].astype(F32) + both[1536:].astype(F32)).astype(BF16)
    chunks = exchange(chunks, ("z", "xh", "xl", "y"))
    grad_piece = jnp.sum(chunks.reshape(8, 8, 48, 128).astype(F32), axis=1).astype(BF16).reshape(384, 128)
    gu_piece = jnp.sum(gu_recv.reshape(4, 4, 96, 128).astype(F32), axis=1).astype(BF16).reshape(384, 128)
    mlp_piece = jnp.concatenate([gu_piece, do_piece], axis=0)
    grad_piece, mlp_far = tie(grad_piece, swap(mlp_piece, "xl"))
    mlp_pair = jnp.stack([mlp_piece, mlp_far])
    mlp_near = [mlp_pair] + [turn(mlp_pair, "y", k) for k in (1, 2, 3)]
    dfirst_part = (dot(dq_keep, w_t) + dot(jnp.concatenate(list(dq_recv), axis=1), w_t_other)).astype(BF16)
    parts = [jnp.concatenate([outs[k], dfirst_part[k * 128 : k * 128 + 128]], axis=0) for k in range(4)]
    parts = [parts[0]] + [turn(parts[k], "z", -k) for k in (1, 2, 3)]
    mine = spread(grad_piece, PLANE, 8)
    total = sum(part.astype(F32) for part in parts)
    block_output = (mixed_own + total[:128]).astype(BF16)[None]
    normed_one, inverse_one = normalize(x_own.astype(F32))
    input_grad = (dmixed + norm_back(total[128:] * gain_one, normed_one, inverse_one)).astype(BF16)[None]

    gate_up_grad, down_grad = call(
        mlp_grad_kernel,
        "mlp_grad",
        (shape(128, 2 * FF, dtype=F32), shape(UNITS, D, dtype=F32)),
        (ids, *mlp_near, *[swap(value, "c") for value in mlp_near]),
    )

    qkv_grad, out_w_grad, qkv_bias_grad, *vectors = call(
        qkv_grad_kernel,
        "qkv_grad",
        (shape(128, 3 * D, dtype=F32), shape(128, D, dtype=F32), shape(1, 384, dtype=F32))
        + (shape(1, 128, dtype=F32),) * 4,
        (ids, mine, swap(mine, "c")),
    )
    vectors = [vector.reshape(128) for vector in vectors]

    return (
        block_output,
        input_grad,
        vectors[0],
        vectors[1],
        qkv_grad,
        qkv_bias_grad.reshape(384),
        out_w_grad,
        vectors[2],
        vectors[3],
        gate_up_grad,
        down_grad,
    )


def solution(mesh):
    fine = jax.sharding.Mesh(mesh.devices.reshape(2, 4, 2, 4, 2), ("xl", "y", "c", "z", "xh"))
    tokens = P(("xl", "y", "c"), SHARD, None)
    rows = P(SHARD, None)
    flat = P(SHARD)
    return jax.shard_map(
        shards,
        mesh=fine,
        in_specs=(tokens, flat, flat, rows, flat, rows, flat, flat, rows, rows, tokens),
        out_specs=(tokens, tokens, flat, flat, rows, flat, rows, flat, flat, rows, rows),
        check_vma=False,
    )
```

profile of v0, /device:TPU:1, one launch (start us, length us, event | category | flops | bytes accessed | tf_op | source)
XLA Modules:
  0.0 275.3 jit_solution(425603598210480110)
XLA Ops:
  5.2 47.1 %all_to_all.35.refs_0_.refs_2_ = bf16[8,1552,128]{2,1,0:T(8,128)(2,1)S(1)} all-to-all(bf16[8,1552,128]{2,1,0:T(8,128)(2,1)S(1)} %pad_maximum_fusion), channel_id=1, replica_groups=mesh['xl'=2,'y'=4,'c'=2,'z'=4,'xh'=2] {'z','xh'}, dimensions={0} | all-to-all | bytes 6356992 | tf_op jit(solution)/shard_map/all_to_all | solution.py:54
  60.1 8.7 %attend_forward.1 = (bf16[384,1024]{1,0:T(8,128)(2,1)}, bf16[8,512,128]{2,1,0:T(8,128)(2,1)}, f32[8,1024]{1,0:T(8,128)}, bf16[384,1024]{1,0:T(8,128)(2,1)}) custom-call(s32[5]{0:T(128)} %stack.44.ids, bf16[8,1552,128]{2,1,0:T(8,128)(2,1)} %copy-done.2, bf16[8,192,128]{2,1,0:T(8,128)(2,1)} %copy-done.21, f32[8,1024]{1,0:T(8,128)} %constant.55.clone.refs_2_.refs_3_, ...), custom_call_target="tpu_custom_call" | custom-call | bytes 1 | tf_op jit(solution)/shard_map/attend_forward/pallas_call | solution.py:165
  71.8 3.6 %all-to-all-start.1 = ((bf16[8,512,128]{2,1,0:T(8,128)(2,1)}), bf16[8,512,128]{2,1,0:T(8,128)(2,1)S(1)}, u32[]{:S(2)}, u32[]{:S(2)}) async-start(bf16[8,512,128]{2,1,0:T(8,128)(2,1)} %get-tuple-element.64), calls=%async_computation.1 | async-start | bytes 2097152 | tf_op jit(solution)/shard_map/all_to_all | solution.py:54
  78.2 8.2 %collective-permute-done.2.refs_2_ = bf16[8,320,128]{2,1,0:T(8,128)(2,1)} collective-permute-done((bf16[8,320,128]{2,1,0:T(8,128)(2,1)S(1)}, bf16[8,320,128]{2,1,0:T(8,128)(2,1)}, u32[]{:S(2)}, u32[]{:S(2)}) %collective-permute-start.2) | collective-permute-done | bytes 655392 | tf_op jit(solution)/shard_map/ppermute | solution.py:66
  91.6 4.7 %normed_input.1.refs_5_ = bf16[1024,1024]{1,0:T(8,128)(2,1)} custom-call(s32[5]{0:T(128)} %stack.44.ids, bf16[8,1552,128]{2,1,0:T(8,128)(2,1)} %copy-done.2), custom_call_target="tpu_custom_call" | custom-call | bytes 1 | tf_op jit(solution)/shard_map/normed_input/pallas_call | solution.py:165
  96.4 5.9 %weights.1 = (bf16[1024,768]{1,0:T(8,128)(2,1)}, bf16[1024,768]{1,0:T(8,128)(2,1)}, bf16[1024,1024]{1,0:T(8,128)(2,1)}) custom-call(s32[5]{0:T(128)} %stack.44.ids, bf16[8,320,128]{2,1,0:T(8,128)(2,1)} %copy-done.11, bf16[8,320,128]{2,1,0:T(8,128)(2,1)} %collective-permute-done.refs_1_, bf16[8,320,128]{2,1,0:T(8,128)(2,1)} %collective-permute-done.2.refs_2_, ...), custom_call_target="tpu_custom_call" | custom-call | bytes 1 | tf_op jit(solution)/shard_map/weights/pallas_call | solution.py:165
  107.1 27.9 %mlp.1 = (f32[128,1024]{1,0:T(8,128)}, bf16[512,1024]{1,0:T(8,128)(2,1)}, f32[8,1024]{1,0:T(8,128)}, bf16[4,128,1024]{2,1,0:T(8,128)(2,1)}, bf16[4,2240,128]{2,1...) custom-call(s32[5]{0:T(128)} %stack.44.ids, ...), custom_call_target="tpu_custom_call" | custom-call | bytes 1 | tf_op jit(solution)/shard_map/mlp/pallas_call | solution.py:165
  136.0 3.9 %all-to-all-start.2 = ((bf16[4,128,1024]{2,1,0:T(8,128)(2,1)}), bf16[4,128,1024]{2,1,0:T(8,128)(2,1)S(1)}, u32[]{:S(2)}, u32[]{:S(2)}) async-start(bf16[4,128,1024]{2,1,0:T(8,128)(2,1)} %get-tuple-element.71), calls=%async_computation.2 | async-start | bytes 2097152 | tf_op jit(solution)/shard_map/all_to_all | solution.py:54
  140.4 2.9 %add_convert_fusion = bf16[4,2240,128]{2,1,0:T(8,128)(2,1)S(1)} fusion(bf16[4,2240,128]{2,1,0:T(8,128)(2,1)} %collective-permute-done.12, bf16[4,2240,128]{2,1,0:T(8,128)(2,1)} %get-tuple-element.82), kind=kLoop, calls=%fused_computation | loop fusion | flops 4587520 | bytes 6881280 | tf_op jit(solution)/shard_map/convert_element_type | solution.py:676
  148.5 6.4 %all-to-all-done.2.refs_0_ = bf16[4,128,1024]{2,1,0:T(8,128)(2,1)S(1)} async-done(((bf16[4,128,1024]{2,1,0:T(8,128)(2,1)}), bf16[4,128,1024]{2,1,0:T(8,128)(2,1)S(1)}, u32[]{:S(2)}, u32[]{:S(2)}) %all-to-all-start.2) | async-done | bytes 1048608 | tf_op jit(solution)/shard_map/all_to_all | solution.py:54
  155.8 4.6 %norm_backward.1 = (f32[128,1024]{1,0:T(8,128)}, bf16[8,384,128]{2,1,0:T(8,128)(2,1)}) custom-call(s32[5]{0:T(128)} %stack.44.ids, bf16[4,128,1024]{2,1,0:T(8,128)(2,1)} %copy-done.5, bf16[128,1024]{1,0:T(8,128)(2,1)} %bitcast.113, f32[128,1024]{1,0:T(8,128)} %get-tuple-element.69.refs_2_, f32[1,1024]{1,0:T(1,128)} %get-tuple-element.125.refs_5_.refs_3_, ...), custom_call_target="tpu_custom_call" | custom-call | bytes 1 | tf_op jit(solution)/shard_map/norm_backward/pallas_call | solution.py:165
  160.4 3.6 %all-to-all-start.3 = ((bf16[8,384,128]{2,1,0:T(8,128)(2,1)}), bf16[8,384,128]{2,1,0:T(8,128)(2,1)S(1)}, u32[]{:S(2)}, u32[]{:S(2)}) async-start(bf16[8,384,128]{2,1,0:T(8,128)(2,1)} %get-tuple-element.72), calls=%async_computation.3 | async-start | bytes 1572864 | tf_op jit(solution)/shard_map/all_to_all | solution.py:54
  164.0 12.4 %collective-permute-done.15 = bf16[2240,128]{1,0:T(8,128)(2,1)} collective-permute-done((bf16[2240,128]{1,0:T(8,128)(2,1)S(1)}, bf16[2240,128]{1,0:T(8,128)(2,1)}, u32[]{:S(2)}, u32[]{:S(2)}) %collective-permute-start.15) | collective-permute-done | bytes 573472 | tf_op jit(solution)/shard_map/ppermute | solution.py:66
  179.2 4.9 %all-to-all-start.4 = ((bf16[16,96,128]{2,1,0:T(8,128)(2,1)}), bf16[16,96,128]{2,1,0:T(8,128)(2,1)S(1)}, u32[]{:S(2)}, u32[]{:S(2)}) async-start(bf16[16,96,128]{2,1,0:T(8,128)(2,1)} %bitcast.30), calls=%async_computation.4 | async-start | bytes 786432 | tf_op jit(solution)/shard_map/all_to_all | solution.py:54
  184.1 12.0 %attend_backward.1 = (bf16[64,48,128]{2,1,0:T(8,128)(2,1)}, bf16[64,48,128]{2,1,0:T(8,128)(2,1)}, bf16[512,384]{1,0:T(8,128)(2,1)}, bf16[1536,128]{1,0:T(8,128)(2,1)}) custom-call(s32[5]{0:T(128)} %stack.44.ids, bf16[8,384,128]{2,1,0:T(8,128)(2,1)} %copy-done.8, bf16[384,1024]{1,0:T(8,128)(2,1)} %get-tuple-element.73.refs_1_, ...), custom_call_target="tpu_custom_call" | custom-call | bytes 1 | tf_op jit(solution)/shard_map/attend_backward/pallas_call | solution.py:165
  201.4 3.2 %collective-permute-start.18 = (bf16[1888,128]{1,0:T(8,128)(2,1)S(1)}, bf16[1888,128]{1,0:T(8,128)(2,1)S(1)}, u32[]{:S(2)}, u32[]{:S(2)}) collective-permute-start(bf16[1888,128]{1,0:T(8,128)(2,1)S(1)} %pad_maximum_fusion.4), channel_id=1, source_target_pairs={{0,1},{1,0},{2,3},{3,2},{4,5},{5,4},{6,7},{7,6},{8,9},{9,8},{10,11... | collective-permute-start | bytes 1449992 | tf_op jit(solution)/shard_map/ppermute | solution.py:62
  204.8 6.5 %all-to-all-start.5 = ((bf16[64,48,128]{2,1,0:T(8,128)(2,1)}), bf16[64,48,128]{2,1,0:T(8,128)(2,1)S(1)}, u32[]{:S(2)}, u32[]{:S(2)}) async-start(bf16[64,48,128]{2,1,0:T(8,128)(2,1)} %add_convert_fusion.2), calls=%async_computation.5 | async-start | bytes 1572864 | tf_op jit(solution)/shard_map/all_to_all | solution.py:54
  211.3 4.3 %collective-permute-done.18 = bf16[1888,128]{1,0:T(8,128)(2,1)S(1)} collective-permute-done((bf16[1888,128]{1,0:T(8,128)(2,1)S(1)}, bf16[1888,128]{1,0:T(8,128)(2,1)S(1)}, u32[]{:S(2)}, u32[]{:S(2)}) %collective-permute-start.18) | collective-permute-done | bytes 483360 | tf_op jit(solution)/shard_map/ppermute | solution.py:62
  229.3 3.5 %all-to-all-start.6 = ((bf16[8,384,128]{2,1,0:T(8,128)(2,1)}), bf16[8,384,128]{2,1,0:T(8,128)(2,1)S(1)}, u32[]{:S(2)}, u32[]{:S(2)}) async-start(bf16[8,384,128]{2,1,0:T(8,128)(2,1)} %broadcast_in_dim.47), calls=%async_computation.6 | async-start | bytes 1572864 | tf_op jit(solution)/shard_map/all_to_all | solution.py:54
  239.2 4.7 %collective-permute-start.27 = (bf16[2,736,128]{2,1,0:T(8,128)(2,1)S(1)}, bf16[2,736,128]{2,1,0:T(8,128)(2,1)}, u32[]{:S(2)}, u32[]{:S(2)}) collective-permute-start(bf16[2,736,128]{2,1,0:T(8,128)(2,1)S(1)} %pad_maximum_fusion.5.refs_0_), channel_id=1, source_target_pairs={{0,8},{8,0},{1,9},{9,1},{2,10},{10,2},{3,11},{11,3},{4,12},{12,4},... | collective-permute-start | bytes 1130504 | tf_op jit(solution)/shard_map/ppermute | solution.py:62
  243.9 7.8 %collective-permute-done.21 = bf16[256,1024]{1,0:T(8,128)(2,1)} collective-permute-done((bf16[256,1024]{1,0:T(8,128)(2,1)}, bf16[256,1024]{1,0:T(8,128)(2,1)}, u32[]{:S(2)}, u32[]{:S(2)}) %collective-permute-start.21) | collective-permute-done | bytes 524320 | tf_op jit(solution)/shard_map/ppermute | solution.py:66
  255.7 4.1 %collective-permute-done.25.refs_2_ = bf16[2,736,128]{2,1,0:T(8,128)(2,1)} collective-permute-done((bf16[2,736,128]{2,1,0:T(8,128)(2,1)S(1)}, bf16[2,736,128]{2,1,0:T(8,128)(2,1)}, u32[]{:S(2)}, u32[]{:S(2)}) %collective-permute-start.25) | collective-permute-done | bytes 376864 | tf_op jit(solution)/shard_map/ppermute | solution.py:66
  265.4 4.9 %mlp_grad.1 = (f32[128,5632]{1,0:T(8,128)}, f32[352,1024]{1,0:T(8,128)}) custom-call(s32[5]{0:T(128)} %stack.44.ids, bf16[2,736,128]{2,1,0:T(8,128)(2,1)} %copy-done.15, bf16[2,736,128]{2,1,0:T(8,128)(2,1)} %collective-permute-done.24.refs_1_, bf16[2,736,128]{2,1,0:T(8,128)(2,1)} %collective-permute-done.25.refs_2_, ...), custom_call_target="tpu_custom_call" | custom-call | bytes 1 | tf_op jit(solution)/shard_map/mlp_grad/pallas_call | solution.py:165
  270.3 3.5 %qkv_grad.1 = (f32[128,3072]{1,0:T(8,128)}, f32[128,1024]{1,0:T(8,128)}, f32[1,384]{1,0:T(1,128)}, f32[1,128]{1,0:T(1,128)}, f32[1,128]{1,0:T(1,128)}, /*index=5*/f32[1,128]{1,0:T(1,128)}, f32[1,128]{1,0:T(1,128)}) custom-call(s32[5]{0:T(128)} %stack.44.ids, bf16[8,384,128]{2,1,0:T(8,128)(2,1)} %copy-done.7, bf16[8,384,128]{2,1,0:T(8,128)(2,1)} %collective-permute-done.23.refs_1_), custom_call_target="tpu_custom_call" | custom-call | bytes 1 | tf_op jit(solution)/shard_map/qkv_grad/pallas_call | solution.py:165
  (187 shorter events, 74.4 us)
Async XLA Ops:
  52.4 18.9 %collective-permute-start = (bf16[8,320,128]{2,1,0:T(8,128)(2,1)S(1)}, bf16[8,320,128]{2,1,0:T(8,128)(2,1)}, u32[]{:S(2)}, u32[]{:S(2)}) collective-permute-start(bf16[8,320,128]{2,1,0:T(8,128)(2,1)S(1)} %slice.74.refs_0_), channel_id=1, source_target_pairs={{0,16},{16,32},{32,48},{48,0},{1,17},{17,33},{33,49},{49,1},{2,18}... | collective-permute-start | bytes 1966088 | tf_op jit(solution)/shard_map/ppermute | solution.py:66
  53.7 17.5 %collective-permute-start.3 = (bf16[8,320,128]{2,1,0:T(8,128)(2,1)S(1)}, bf16[8,320,128]{2,1,0:T(8,128)(2,1)}, u32[]{:S(2)}, u32[]{:S(2)}) collective-permute-start(bf16[8,320,128]{2,1,0:T(8,128)(2,1)S(1)} %slice.74.refs_0_), channel_id=1, source_target_pairs={{0,48},{16,0},{32,16},{48,32},{1,49},{17,1},{33,17},{49,33},{2,50}... | collective-permute-start | bytes 1966088 | tf_op jit(solution)/shard_map/ppermute | solution.py:66
  68.8 17.6 %collective-permute-start.2 = (bf16[8,320,128]{2,1,0:T(8,128)(2,1)S(1)}, bf16[8,320,128]{2,1,0:T(8,128)(2,1)}, u32[]{:S(2)}, u32[]{:S(2)}) collective-permute-start(bf16[8,320,128]{2,1,0:T(8,128)(2,1)S(1)} %slice.74.refs_0_), channel_id=1, source_target_pairs={{0,32},{16,48},{32,0},{48,16},{1,33},{17,49},{33,1},{49,17},{2,34}... | collective-permute-start | bytes 1966088 | tf_op jit(solution)/shard_map/ppermute | solution.py:66
  70.6 17.1 %collective-permute-start.4 = (bf16[8,320,128]{2,1,0:T(8,128)(2,1)S(1)}, bf16[8,320,128]{2,1,0:T(8,128)(2,1)}, u32[]{:S(2)}, u32[]{:S(2)}) collective-permute-start(bf16[8,320,128]{2,1,0:T(8,128)(2,1)S(1)} %slice.74.refs_0_), channel_id=1, source_target_pairs={{0,8},{8,0},{1,9},{9,1},{2,10},{10,2},{3,11},{11,3},{4,12},{12,4},... | collective-permute-start | bytes 1966088 | tf_op jit(solution)/shard_map/ppermute | solution.py:62
  71.2 17.3 %collective-permute-start.5 = (bf16[8,320,128]{2,1,0:T(8,128)(2,1)}, bf16[8,320,128]{2,1,0:T(8,128)(2,1)}, u32[]{:S(2)}, u32[]{:S(2)}) collective-permute-start(bf16[8,320,128]{2,1,0:T(8,128)(2,1)} %collective-permute-done.refs_1_), channel_id=1, source_target_pairs={{0,8},{8,0},{1,9},{9,1},{2,10},{10,2},{3,11},{11,3},{4,12},{12,4},... | collective-permute-start | bytes 1966088 | tf_op jit(solution)/shard_map/ppermute | solution.py:62
  71.3 17.9 %collective-permute-start.7 = (bf16[8,320,128]{2,1,0:T(8,128)(2,1)}, bf16[8,320,128]{2,1,0:T(8,128)(2,1)}, u32[]{:S(2)}, u32[]{:S(2)}) collective-permute-start(bf16[8,320,128]{2,1,0:T(8,128)(2,1)} %collective-permute-done.3.refs_3_), channel_id=1, source_target_pairs={{0,8},{8,0},{1,9},{9,1},{2,10},{10,2},{3,11},{11,3},{4,12},{12,4},... | collective-permute-start | bytes 1966088 | tf_op jit(solution)/shard_map/ppermute | solution.py:62
  71.8 34.3 %all-to-all-start.1 = ((bf16[8,512,128]{2,1,0:T(8,128)(2,1)}), bf16[8,512,128]{2,1,0:T(8,128)(2,1)S(1)}, u32[]{:S(2)}, u32[]{:S(2)}) async-start(bf16[8,512,128]{2,1,0:T(8,128)(2,1)} %get-tuple-element.64), calls=%async_computation.1 | async-start | bytes 2097152 | tf_op jit(solution)/shard_map/all_to_all | solution.py:54
  75.3 30.8 %collective-permute-start.11 = (bf16[352,1024]{1,0:T(8,128)(2,1)S(1)}, bf16[352,1024]{1,0:T(8,128)(2,1)}, u32[]{:S(2)}, u32[]{:S(2)}) collective-permute-start(bf16[352,1024]{1,0:T(8,128)(2,1)S(1)} %copy-done.18), channel_id=1, source_target_pairs={{0,1},{1,0},{2,3},{3,2},{4,5},{5,4},{6,7},{7,6},{8,9},{9,8},{10,11... | collective-permute-start | bytes 2162696 | tf_op jit(solution)/shard_map/ppermute | solution.py:62
  136.0 18.9 %all-to-all-start.2 = ((bf16[4,128,1024]{2,1,0:T(8,128)(2,1)}), bf16[4,128,1024]{2,1,0:T(8,128)(2,1)S(1)}, u32[]{:S(2)}, u32[]{:S(2)}) async-start(bf16[4,128,1024]{2,1,0:T(8,128)(2,1)} %get-tuple-element.71), calls=%async_computation.2 | async-start | bytes 2097152 | tf_op jit(solution)/shard_map/all_to_all | solution.py:54
  145.6 18.4 %collective-permute-start.13 = (bf16[2240,128]{1,0:T(8,128)(2,1)}, bf16[2240,128]{1,0:T(8,128)(2,1)}, u32[]{:S(2)}, u32[]{:S(2)}) collective-permute-start(bf16[2240,128]{1,0:T(8,128)(2,1)} %get-tuple-element.107), channel_id=1, source_target_pairs={{0,48},{16,0},{32,16},{48,32},{1,49},{17,1},{33,17},{49,33},{2,50}... | collective-permute-start | bytes 1720328 | tf_op jit(solution)/shard_map/ppermute | solution.py:66
  147.6 16.4 %collective-permute-start.14 = (bf16[2240,128]{1,0:T(8,128)(2,1)S(1)}, bf16[2240,128]{1,0:T(8,128)(2,1)}, u32[]{:S(2)}, u32[]{:S(2)}) collective-permute-start(bf16[2240,128]{1,0:T(8,128)(2,1)S(1)} %get-tuple-element.109), channel_id=1, source_target_pairs={{0,32},{16,48},{32,0},{48,16},{1,33},{17,49},{33,1},{49,17},{2,34}... | collective-permute-start | bytes 1720328 | tf_op jit(solution)/shard_map/ppermute | solution.py:66
  148.0 28.5 %collective-permute-start.15 = (bf16[2240,128]{1,0:T(8,128)(2,1)S(1)}, bf16[2240,128]{1,0:T(8,128)(2,1)}, u32[]{:S(2)}, u32[]{:S(2)}) collective-permute-start(bf16[2240,128]{1,0:T(8,128)(2,1)S(1)} %get-tuple-element.108), channel_id=1, source_target_pairs={{0,16},{16,32},{32,48},{48,0},{1,17},{17,33},{33,49},{49,1},{2,18}... | collective-permute-start | bytes 1720328 | tf_op jit(solution)/shard_map/ppermute | solution.py:66
  148.4 47.7 %collective-permute-start.16 = (bf16[384,1024]{1,0:T(8,128)(2,1)S(1)}, bf16[384,1024]{1,0:T(8,128)(2,1)}, u32[]{:S(2)}, u32[]{:S(2)}) collective-permute-start(bf16[384,1024]{1,0:T(8,128)(2,1)S(1)} %copy-done.9), channel_id=1, source_target_pairs={{0,1},{1,0},{2,3},{3,2},{4,5},{5,4},{6,7},{7,6},{8,9},{9,8},{10,11... | collective-permute-start | bytes 2359304 | tf_op jit(solution)/shard_map/ppermute | solution.py:62
  160.4 18.7 %all-to-all-start.3 = ((bf16[8,384,128]{2,1,0:T(8,128)(2,1)}), bf16[8,384,128]{2,1,0:T(8,128)(2,1)S(1)}, u32[]{:S(2)}, u32[]{:S(2)}) async-start(bf16[8,384,128]{2,1,0:T(8,128)(2,1)} %get-tuple-element.72), calls=%async_computation.3 | async-start | bytes 1572864 | tf_op jit(solution)/shard_map/all_to_all | solution.py:54
  179.2 17.0 %all-to-all-start.4 = ((bf16[16,96,128]{2,1,0:T(8,128)(2,1)}), bf16[16,96,128]{2,1,0:T(8,128)(2,1)S(1)}, u32[]{:S(2)}, u32[]{:S(2)}) async-start(bf16[16,96,128]{2,1,0:T(8,128)(2,1)} %bitcast.30), calls=%async_computation.4 | async-start | bytes 786432 | tf_op jit(solution)/shard_map/all_to_all | solution.py:54
  204.8 22.6 %all-to-all-start.5 = ((bf16[64,48,128]{2,1,0:T(8,128)(2,1)}), bf16[64,48,128]{2,1,0:T(8,128)(2,1)S(1)}, u32[]{:S(2)}, u32[]{:S(2)}) async-start(bf16[64,48,128]{2,1,0:T(8,128)(2,1)} %add_convert_fusion.2), calls=%async_computation.5 | async-start | bytes 1572864 | tf_op jit(solution)/shard_map/all_to_all | solution.py:54
  221.4 16.6 %collective-permute-start.19 = (bf16[256,1024]{1,0:T(8,128)(2,1)}, bf16[256,1024]{1,0:T(8,128)(2,1)}, u32[]{:S(2)}, u32[]{:S(2)}) collective-permute-start(bf16[256,1024]{1,0:T(8,128)(2,1)} %pad_maximum_fusion.1), channel_id=1, source_target_pairs={{0,6},{2,0},{4,2},{6,4},{1,7},{3,1},{5,3},{7,5},{8,14},{10,8},{12,... | collective-permute-start | bytes 1572872 | tf_op jit(solution)/shard_map/ppermute | solution.py:66
  226.1 25.6 %collective-permute-start.21 = (bf16[256,1024]{1,0:T(8,128)(2,1)}, bf16[256,1024]{1,0:T(8,128)(2,1)}, u32[]{:S(2)}, u32[]{:S(2)}) collective-permute-start(bf16[256,1024]{1,0:T(8,128)(2,1)} %pad_maximum_fusion.3), channel_id=1, source_target_pairs={{0,2},{2,4},{4,6},{6,0},{1,3},{3,5},{5,7},{7,1},{8,10},{10,12},{12... | collective-permute-start | bytes 1572872 | tf_op jit(solution)/shard_map/ppermute | solution.py:66
  229.3 22.4 %all-to-all-start.6 = ((bf16[8,384,128]{2,1,0:T(8,128)(2,1)}), bf16[8,384,128]{2,1,0:T(8,128)(2,1)S(1)}, u32[]{:S(2)}, u32[]{:S(2)}) async-start(bf16[8,384,128]{2,1,0:T(8,128)(2,1)} %broadcast_in_dim.47), calls=%async_computation.6 | async-start | bytes 1572864 | tf_op jit(solution)/shard_map/all_to_all | solution.py:54
  234.2 20.0 %collective-permute-start.24 = (bf16[2,736,128]{2,1,0:T(8,128)(2,1)S(1)}, bf16[2,736,128]{2,1,0:T(8,128)(2,1)}, u32[]{:S(2)}, u32[]{:S(2)}) collective-permute-start(bf16[2,736,128]{2,1,0:T(8,128)(2,1)S(1)} %pad_maximum_fusion.5.refs_0_), channel_id=1, source_target_pairs={{0,16},{16,32},{32,48},{48,0},{1,17},{17,33},{33,49},{49,1},{2,18}... | collective-permute-start | bytes 1130504 | tf_op jit(solution)/shard_map/ppermute | solution.py:66
  235.6 24.2 %collective-permute-start.25 = (bf16[2,736,128]{2,1,0:T(8,128)(2,1)S(1)}, bf16[2,736,128]{2,1,0:T(8,128)(2,1)}, u32[]{:S(2)}, u32[]{:S(2)}) collective-permute-start(bf16[2,736,128]{2,1,0:T(8,128)(2,1)S(1)} %pad_maximum_fusion.5.refs_0_), channel_id=1, source_target_pairs={{0,32},{16,48},{32,0},{48,16},{1,33},{17,49},{33,1},{49,17},{2,34}... | collective-permute-start | bytes 1130504 | tf_op jit(solution)/shard_map/ppermute | solution.py:66
  238.0 24.3 %collective-permute-start.26 = (bf16[2,736,128]{2,1,0:T(8,128)(2,1)S(1)}, bf16[2,736,128]{2,1,0:T(8,128)(2,1)}, u32[]{:S(2)}, u32[]{:S(2)}) collective-permute-start(bf16[2,736,128]{2,1,0:T(8,128)(2,1)S(1)} %pad_maximum_fusion.5.refs_0_), channel_id=1, source_target_pairs={{0,48},{16,0},{32,16},{48,32},{1,49},{17,1},{33,17},{49,33},{2,50}... | collective-permute-start | bytes 1130504 | tf_op jit(solution)/shard_map/ppermute | solution.py:66
  239.2 25.4 %collective-permute-start.27 = (bf16[2,736,128]{2,1,0:T(8,128)(2,1)S(1)}, bf16[2,736,128]{2,1,0:T(8,128)(2,1)}, u32[]{:S(2)}, u32[]{:S(2)}) collective-permute-start(bf16[2,736,128]{2,1,0:T(8,128)(2,1)S(1)} %pad_maximum_fusion.5.refs_0_), channel_id=1, source_target_pairs={{0,8},{8,0},{1,9},{9,1},{2,10},{10,2},{3,11},{11,3},{4,12},{12,4},... | collective-permute-start | bytes 1130504 | tf_op jit(solution)/shard_map/ppermute | solution.py:62
  251.7 18.6 %collective-permute-start.23 = (bf16[8,384,128]{2,1,0:T(8,128)(2,1)S(1)}, bf16[8,384,128]{2,1,0:T(8,128)(2,1)}, u32[]{:S(2)}, u32[]{:S(2)}) collective-permute-start(bf16[8,384,128]{2,1,0:T(8,128)(2,1)S(1)} %all-to-all-done.6.refs_0_), channel_id=1, source_target_pairs={{0,8},{8,0},{1,9},{9,1},{2,10},{10,2},{3,11},{11,3},{4,12},{12,4},... | collective-permute-start | bytes 2359304 | tf_op jit(solution)/shard_map/ppermute | solution.py:62
  (50 other events, 384.6 us)
where the time goes:
time: 279 us; the launch traced here: 275 us
  Pallas kernels  72.2 us (26%)
  starting transfers between devices  68.5 us (25%)
  waiting for transfers between devices  51.8 us (19%)
  blocking collectives  47.1 us (17%)
  other arithmetic  18.3 us (7%)
  local copies, waits for them, and re-layouts  13.2 us (5%)
    pallas_call x8, Pallas kernels, call(): pl.pallas_call(body, out_shape=out_shape, in_specs=[pl.BlockSpec(memory_s...  72.2 us
    all_to_all x1, blocking collectives, exchange(): return lax.all_to_all(value, axes, 0, 0, tiled=True)  47.1 us
    ppermute x15, waiting for transfers between devices, turn(): return lax.ppermute(value, axis, [(i, (i + step) % 4) for i in range(4)])  34.8 us
    all_to_all x6, starting transfers between devices, exchange(): return lax.all_to_all(value, axes, 0, 0, tiled=True)  25.9 us
    ppermute x16, starting transfers between devices, swap(): return lax.ppermute(value, axis, [(0, 1), (1, 0)])  23.7 us
    ppermute x15, starting transfers between devices, turn(): return lax.ppermute(value, axis, [(i, (i + step) % 4) for i in range(4)])  18.8 us
    ppermute x16, waiting for transfers between devices, swap(): return lax.ppermute(value, axis, [(0, 1), (1, 0)])  10.1 us
    all_to_all x6, waiting for transfers between devices, exchange(): return lax.all_to_all(value, axes, 0, 0, tiled=True)  6.97 us
  transfers between devices with their start and end apart: 37, of which 13 were waited for; matrix products, arithmetic and copies ran while one was open for 8% of the time, Pallas kernels for 15%

commit v1 on v0

--- a/solution.py
+++ b/solution.py
@@ -503,9 +503,9 @@
         return lax.rem(xl + i, 2), lax.rem(y - k + 4, 4)
 
     def wide(ref, i, z, which):
-        at = z * 96 + which * 48
+        at = i * 384 + z * 96 + which * 48
         return jnp.concatenate(
-            [ref[i, at + cb * 16 : at + cb * 16 + 16, :].astype(F32) for cb in range(3)], axis=1
+            [ref[at + cb * 16 : at + cb * 16 + 16, :].astype(F32) for cb in range(3)], axis=1
         )[:, :UNITS]
 
     for k in range(4):
@@ -522,10 +522,10 @@
     for refs, half in ((mine, c), (other, 1 - c)):
         for k in range(4):
             lanes = pl.ds(pl.multiple_of(half * 512 + place(k, 0)[1] * 128, 128), 128)
-            down[:, lanes] = refs[k][0, 384:736, :].astype(F32) + refs[k][1, 384:736, :].astype(F32)
-
-
-def qkv_grad_kernel(ids, mine, other, qkv, out_w, qkv_bias, attn_gain, attn_bias, mlp_gain, mlp_bias):
+            down[:, lanes] = refs[k][768:1120, :].astype(F32)
+
+
+def last_kernel(ids, mine, other, qkv, out_w, qkv_bias, attn_gain, attn_bias, mlp_gain, mlp_bias):
     c = ids[ID_C]
     s = ids[ID_Z] * 2 + ids[ID_XH]
     totals = []
@@ -555,7 +555,7 @@
         for src in range(8):
             for kind in range(3):
                 found += jnp.where(block == 8 * kind + src, totals[4 + kind][src], 0.0)
-        qkv_bias[:, i * 128 : i * 128 + 128] = found
+        qkv_bias[i * 128 : i * 128 + 128] = found.reshape(128)
 
 
 def shards(
@@ -615,10 +615,11 @@
         (ids, head_of(packet), qkv_other, cos, sin),
         scratch=[pltpu.VMEM((D, 384), BF16)],
     )
-    att_blocks, packet_late, far, dy_now = tie(att_blocks, packet, piece, dy_own)
+    att_blocks, packet_late, dy_now, far = tie(att_blocks, packet, dy_own, piece)
+    att = exchange(att_blocks, SHARD)
+    dy_now, before, after, down_other = tie(dy_now, before, after, down_other)
+    dys = [dy_now] + [turn(dy_now, "z", k) for k in (1, 2, 3)]
     pieces = [piece, before, turn(far, "y", 2), after]
-    dys = [dy_now] + [turn(dy_now, "z", k) for k in (1, 2, 3)]
-    att = exchange(att_blocks, SHARD)
     (xhat,) = call(
         normed_kernel,
         "normed_input",
@@ -633,9 +634,9 @@
         (ids, *pieces),
     )
 
+    out_w, xhat = tie(out_w, xhat)
     vecs = packet[:, VEC_AT : VEC_AT + 4].astype(F32).transpose(1, 0, 2).reshape(4, 1, D)
     gain_one, bias_one, gain_two, bias_two = vecs[0], vecs[1], vecs[2], vecs[3]
-    out_w, xhat = tie(out_w, xhat)
     w_t_other = swap(w_t, "xh")
 
     mixed_own, att_rel, mlp_small, ds, keep, send, *outs = call(
@@ -705,39 +706,51 @@
     gu_recv = exchange(mlp_y[:1536].reshape(16, 96, 128), ("z", "xh", "xl"))
     grad_send, gu_recv, w_t_other = tie(grad_send, gu_recv, w_t_other)
     chunks = (grad_keep.astype(F32) + swap(grad_send, "c").astype(F32)).astype(BF16)
+    gu_piece = jnp.sum(gu_recv.reshape(4, 4, 96, 128).astype(F32), axis=1).astype(BF16).reshape(384, 128)
+    do_own, do_send = mlp_y[1536:1888], mlp_y[1888:2240]
     chunks, dq_send = tie(chunks, dq_send)
-    both = swap(jnp.concatenate([dq_send, mlp_y[1888:2240]], axis=0), "xh")
+    both = swap(jnp.concatenate([dq_send, do_send], axis=0), "xh")
     dq_recv = both[:1536].reshape(3, 512, 128)
-    do_piece = (mlp_y[1536:1888].astype(F32) + both[1536:].astype(F32)).astype(BF16)
     chunks = exchange(chunks, ("z", "xh", "xl", "y"))
     grad_piece = jnp.sum(chunks.reshape(8, 8, 48, 128).astype(F32), axis=1).astype(BF16).reshape(384, 128)
-    gu_piece = jnp.sum(gu_recv.reshape(4, 4, 96, 128).astype(F32), axis=1).astype(BF16).reshape(384, 128)
-    mlp_piece = jnp.concatenate([gu_piece, do_piece], axis=0)
-    grad_piece, mlp_far = tie(grad_piece, swap(mlp_piece, "xl"))
-    mlp_pair = jnp.stack([mlp_piece, mlp_far])
-    mlp_near = [mlp_pair] + [turn(mlp_pair, "y", k) for k in (1, 2, 3)]
-    dfirst_part = (dot(dq_keep, w_t) + dot(jnp.concatenate(list(dq_recv), axis=1), w_t_other)).astype(BF16)
-    parts = [jnp.concatenate([outs[k], dfirst_part[k * 128 : k * 128 + 128]], axis=0) for k in range(4)]
+    do_half = (do_own.astype(F32) + both[1536:].astype(F32)).astype(BF16)
+    gu_far, do_far = swap(gu_piece, "xl"), swap(do_half, "xl")
+    do_piece = (do_half.astype(F32) + do_far.astype(F32)).astype(BF16)
+    mlp_piece = jnp.concatenate([gu_piece, gu_far, do_piece], axis=0)
+    grad_piece, mlp_piece = tie(grad_piece, mlp_piece)
+    mlp_near = [mlp_piece] + [turn(mlp_piece, "y", k) for k in (1, 2, 3)]
+
+    dfirst_part = (
+        dot(dq_keep, w_t) + dot(jnp.concatenate(list(dq_recv), axis=1), w_t_other)
+    ).astype(BF16)
+    parts = [dfirst_part[k * 128 : k * 128 + 128] for k in range(4)]
+    parts = [jnp.concatenate([outs[k], parts[k]], axis=0) for k in range(4)]
     parts = [parts[0]] + [turn(parts[k], "z", -k) for k in (1, 2, 3)]
     mine = spread(grad_piece, PLANE, 8)
     total = sum(part.astype(F32) for part in parts)
     block_output = (mixed_own + total[:128]).astype(BF16)[None]
+    total = total[128:]
     normed_one, inverse_one = normalize(x_own.astype(F32))
-    input_grad = (dmixed + norm_back(total[128:] * gain_one, normed_one, inverse_one)).astype(BF16)[None]
-
+    input_grad = (dmixed + norm_back(total * gain_one, normed_one, inverse_one)).astype(BF16)[None]
+
+    qkv_grad, out_w_grad, qkv_bias_grad, *vectors = call(
+        last_kernel,
+        "last",
+        (
+            shape(128, 3 * D, dtype=F32),
+            shape(128, D, dtype=F32),
+            shape(384, dtype=F32),
+        )
+        + (shape(1, 128, dtype=F32),) * 4,
+        (ids, mine, swap(mine, "c")),
+    )
+    mlp_theirs = [swap(value, "c") for value in mlp_near]
+    qkv_grad, input_grad, *mlp_theirs = tie(qkv_grad, input_grad, *mlp_theirs)
     gate_up_grad, down_grad = call(
         mlp_grad_kernel,
         "mlp_grad",
         (shape(128, 2 * FF, dtype=F32), shape(UNITS, D, dtype=F32)),
-        (ids, *mlp_near, *[swap(value, "c") for value in mlp_near]),
-    )
-
-    qkv_grad, out_w_grad, qkv_bias_grad, *vectors = call(
-        qkv_grad_kernel,
-        "qkv_grad",
-        (shape(128, 3 * D, dtype=F32), shape(128, D, dtype=F32), shape(1, 384, dtype=F32))
-        + (shape(1, 128, dtype=F32),) * 4,
-        (ids, mine, swap(mine, "c")),
+        (ids, *mlp_near, *mlp_theirs),
     )
     vectors = [vector.reshape(128) for vector in vectors]
 
@@ -747,7 +760,7 @@
         vectors[0],
         vectors[1],
         qkv_grad,
-        qkv_bias_grad.reshape(384),
+        qkv_bias_grad,
         out_w_grad,
         vectors[2],
         vectors[3],

time: 279 us -> 274 us (0.982)
  waiting for transfers between devices: 51.8 us -> 47.6 us
    ppermute x15, waiting for transfers between devices: 34.8 us -> 31.9 us  [turn(): return lax.ppermute(value, axis, [(i, (i + step) % 4) for i in range(4)])]
    ppermute x16 -> x17, starting transfers between devices: 23.7 us -> 23.2 us  [swap(): return lax.ppermute(value, axis, [(0, 1), (1, 0)])]
    unnamed x75 -> x73, local copies, waits for them, and re-layouts: 6.02 us -> 5.69 us
    ppermute x16 -> x17, waiting for transfers between devices: 10.1 us -> 10.4 us  [swap(): return lax.ppermute(value, axis, [(0, 1), (1, 0)])]
  transfers between devices with their start and end apart: 37 -> 38, of which waited for: 13 -> 11; matrix products, arithmetic and copies ran while one was open for 8% -> 8% of each run, Pallas kernels for 15% -> 15%
where the time goes in v1:
time: 274 us; the launch traced here: 270 us
  Pallas kernels  72 us (26%)
  starting transfers between devices  69.1 us (25%)
  waiting for transfers between devices  47.6 us (17%)
  blocking collectives  47.2 us (17%)
  other arithmetic  16.5 us (6%)
  local copies, waits for them, and re-layouts  12.9 us (5%)
    pallas_call x8, Pallas kernels, call(): pl.pallas_call(body, out_shape=out_shape, in_specs=[pl.BlockSpec(memory_s...  72 us
    all_to_all x1, blocking collectives, exchange(): return lax.all_to_all(value, axes, 0, 0, tiled=True)  47.2 us
    ppermute x15, waiting for transfers between devices, turn(): return lax.ppermute(value, axis, [(i, (i + step) % 4) for i in range(4)])  31.9 us
    all_to_all x6, starting transfers between devices, exchange(): return lax.all_to_all(value, axes, 0, 0, tiled=True)  26.7 us
    ppermute x17, starting transfers between devices, swap(): return lax.ppermute(value, axis, [(0, 1), (1, 0)])  23.2 us
    ppermute x15, starting transfers between devices, turn(): return lax.ppermute(value, axis, [(i, (i + step) % 4) for i in range(4)])  19.2 us
    ppermute x17, waiting for transfers between devices, swap(): return lax.ppermute(value, axis, [(0, 1), (1, 0)])  10.4 us
    unnamed x73, local copies, waits for them, and re-layouts  5.69 us
  transfers between devices with their start and end apart: 38, of which 11 were waited for; matrix products, arithmetic and copies ran while one was open for 8% of the time, Pallas kernels for 15%

profile of v1, /device:TPU:1, one launch (start us, length us, event | category | flops | bytes accessed | tf_op | source)
XLA Modules:
  0.0 269.6 jit_solution(6629354549067283513)
XLA Ops:
  5.2 47.2 %all_to_all.35.refs_0_.refs_2_ = bf16[8,1552,128]{2,1,0:T(8,128)(2,1)S(1)} all-to-all(bf16[8,1552,128]{2,1,0:T(8,128)(2,1)S(1)} %pad_maximum_fusion), channel_id=1, replica_groups=mesh['xl'=2,'y'=4,'c'=2,'z'=4,'xh'=2] {'z','xh'}, dimensions={0} | all-to-all | bytes 6356992 | tf_op jit(solution)/shard_map/all_to_all | solution.py:54
  56.4 2.9 %collective-permute-start = (bf16[8,192,128]{2,1,0:T(8,128)(2,1)S(1)}, bf16[8,192,128]{2,1,0:T(8,128)(2,1)}, u32[]{:S(2)}, u32[]{:S(2)}) collective-permute-start(bf16[8,192,128]{2,1,0:T(8,128)(2,1)S(1)} %slice.75), channel_id=1, source_target_pairs={{0,8},{8,0},{1,9},{9,1},{2,10},{10,2},{3,11},{11,3},{4,12},{12,4},... | collective-permute-start | bytes 1179656 | tf_op jit(solution)/shard_map/ppermute | solution.py:62
  60.7 8.7 %attend_forward.1 = (bf16[384,1024]{1,0:T(8,128)(2,1)}, bf16[8,512,128]{2,1,0:T(8,128)(2,1)}, f32[8,1024]{1,0:T(8,128)}, bf16[384,1024]{1,0:T(8,128)(2,1)}) custom-call(s32[5]{0:T(128)} %stack.35.ids, bf16[8,1552,128]{2,1,0:T(8,128)(2,1)} %copy-done.2, bf16[8,192,128]{2,1,0:T(8,128)(2,1)} %collective-permute-done.refs_1_, ...), custom_call_target="tpu_custom_call" | custom-call | bytes 1 | tf_op jit(solution)/shard_map/attend_forward/pallas_call | solution.py:165
  72.8 4.1 %all-to-all-start.1 = ((bf16[8,512,128]{2,1,0:T(8,128)(2,1)}), bf16[8,512,128]{2,1,0:T(8,128)(2,1)S(1)}, u32[]{:S(2)}, u32[]{:S(2)}) async-start(bf16[8,512,128]{2,1,0:T(8,128)(2,1)} %get-tuple-element.78), calls=%async_computation.1 | async-start | bytes 2097152 | tf_op jit(solution)/shard_map/all_to_all | solution.py:54
  77.5 9.6 %collective-permute-done.4.refs_2_ = bf16[8,320,128]{2,1,0:T(8,128)(2,1)} collective-permute-done((bf16[8,320,128]{2,1,0:T(8,128)(2,1)S(1)}, bf16[8,320,128]{2,1,0:T(8,128)(2,1)}, u32[]{:S(2)}, u32[]{:S(2)}) %collective-permute-start.4) | collective-permute-done | bytes 655392 | tf_op jit(solution)/shard_map/ppermute | solution.py:66
  92.1 4.8 %normed_input.1.refs_5_ = bf16[1024,1024]{1,0:T(8,128)(2,1)} custom-call(s32[5]{0:T(128)} %stack.35.ids, bf16[8,1552,128]{2,1,0:T(8,128)(2,1)} %copy-done.2), custom_call_target="tpu_custom_call" | custom-call | bytes 1 | tf_op jit(solution)/shard_map/normed_input/pallas_call | solution.py:165
  96.9 5.9 %weights.1 = (bf16[1024,768]{1,0:T(8,128)(2,1)}, bf16[1024,768]{1,0:T(8,128)(2,1)}, bf16[1024,1024]{1,0:T(8,128)(2,1)}) custom-call(s32[5]{0:T(128)} %stack.35.ids, bf16[8,320,128]{2,1,0:T(8,128)(2,1)} %copy-done.11, bf16[8,320,128]{2,1,0:T(8,128)(2,1)} %collective-permute-done.1.refs_1_, bf16[8,320,128]{2,1,0:T(8,128)(2,1)} %collective-permute-done.4.refs_2_, ...), custom_call_target="tpu_custom_call" | custom-call | bytes 1 | tf_op jit(solution)/shard_map/weights/pallas_call | solution.py:165
  106.5 27.8 %mlp.1 = (f32[128,1024]{1,0:T(8,128)}, bf16[512,1024]{1,0:T(8,128)(2,1)}, f32[8,1024]{1,0:T(8,128)}, bf16[4,128,1024]{2,1,0:T(8,128)(2,1)}, bf16[4,2240,128]{2,1...) custom-call(s32[5]{0:T(128)} %stack.35.ids, ...), custom_call_target="tpu_custom_call" | custom-call | bytes 1 | tf_op jit(solution)/shard_map/mlp/pallas_call | solution.py:165
  135.0 3.5 %all-to-all-start.2 = ((bf16[4,128,1024]{2,1,0:T(8,128)(2,1)}), bf16[4,128,1024]{2,1,0:T(8,128)(2,1)S(1)}, u32[]{:S(2)}, u32[]{:S(2)}) async-start(bf16[4,128,1024]{2,1,0:T(8,128)(2,1)} %get-tuple-element.85), calls=%async_computation.2 | async-start | bytes 2097152 | tf_op jit(solution)/shard_map/all_to_all | solution.py:54
  139.4 2.9 %add_convert_fusion = bf16[4,2240,128]{2,1,0:T(8,128)(2,1)S(1)} fusion(bf16[4,2240,128]{2,1,0:T(8,128)(2,1)} %collective-permute-done.12, bf16[4,2240,128]{2,1,0:T(8,128)(2,1)} %get-tuple-element.96), kind=kLoop, calls=%fused_computation | loop fusion | flops 4587520 | bytes 6881280 | tf_op jit(solution)/shard_map/convert_element_type | solution.py:677
  148.4 5.3 %all-to-all-done.2.refs_0_ = bf16[4,128,1024]{2,1,0:T(8,128)(2,1)S(1)} async-done(((bf16[4,128,1024]{2,1,0:T(8,128)(2,1)}), bf16[4,128,1024]{2,1,0:T(8,128)(2,1)S(1)}, u32[]{:S(2)}, u32[]{:S(2)}) %all-to-all-start.2) | async-done | bytes 1048608 | tf_op jit(solution)/shard_map/all_to_all | solution.py:54
  154.8 4.6 %norm_backward.1 = (f32[128,1024]{1,0:T(8,128)}, bf16[8,384,128]{2,1,0:T(8,128)(2,1)}) custom-call(s32[5]{0:T(128)} %stack.35.ids, bf16[4,128,1024]{2,1,0:T(8,128)(2,1)} %copy-done.5, bf16[128,1024]{1,0:T(8,128)(2,1)} %bitcast.110, f32[128,1024]{1,0:T(8,128)} %get-tuple-element.83.refs_2_, f32[1,1024]{1,0:T(1,128)} %get-tuple-element.143.refs_5_.refs_3_, ...), custom_call_target="tpu_custom_call" | custom-call | bytes 1 | tf_op jit(solution)/shard_map/norm_backward/pallas_call | solution.py:165
  159.4 3.6 %all-to-all-start.3 = ((bf16[8,384,128]{2,1,0:T(8,128)(2,1)}), bf16[8,384,128]{2,1,0:T(8,128)(2,1)S(1)}, u32[]{:S(2)}, u32[]{:S(2)}) async-start(bf16[8,384,128]{2,1,0:T(8,128)(2,1)} %get-tuple-element.86), calls=%async_computation.3 | async-start | bytes 1572864 | tf_op jit(solution)/shard_map/all_to_all | solution.py:54
  163.0 12.2 %collective-permute-done.15 = bf16[2240,128]{1,0:T(8,128)(2,1)} collective-permute-done((bf16[2240,128]{1,0:T(8,128)(2,1)S(1)}, bf16[2240,128]{1,0:T(8,128)(2,1)}, u32[]{:S(2)}, u32[]{:S(2)}) %collective-permute-start.15) | collective-permute-done | bytes 573472 | tf_op jit(solution)/shard_map/ppermute | solution.py:66
  177.9 4.5 %all-to-all-start.4 = ((bf16[16,96,128]{2,1,0:T(8,128)(2,1)}), bf16[16,96,128]{2,1,0:T(8,128)(2,1)S(1)}, u32[]{:S(2)}, u32[]{:S(2)}) async-start(bf16[16,96,128]{2,1,0:T(8,128)(2,1)} %bitcast.30), calls=%async_computation.4 | async-start | bytes 786432 | tf_op jit(solution)/shard_map/all_to_all | solution.py:54
  182.4 12.0 %attend_backward.1 = (bf16[64,48,128]{2,1,0:T(8,128)(2,1)}, bf16[64,48,128]{2,1,0:T(8,128)(2,1)}, bf16[512,384]{1,0:T(8,128)(2,1)}, bf16[1536,128]{1,0:T(8,128)(2,1)}) custom-call(s32[5]{0:T(128)} %stack.35.ids, bf16[8,384,128]{2,1,0:T(8,128)(2,1)} %copy-done.8, bf16[384,1024]{1,0:T(8,128)(2,1)} %get-tuple-element.87.refs_1_, ...), custom_call_target="tpu_custom_call" | custom-call | bytes 1 | tf_op jit(solution)/shard_map/attend_backward/pallas_call | solution.py:165
  199.8 3.2 %collective-permute-start.18 = (bf16[1888,128]{1,0:T(8,128)(2,1)S(1)}, bf16[1888,128]{1,0:T(8,128)(2,1)S(1)}, u32[]{:S(2)}, u32[]{:S(2)}) collective-permute-start(bf16[1888,128]{1,0:T(8,128)(2,1)S(1)} %pad_maximum_fusion.4), channel_id=1, source_target_pairs={{0,1},{1,0},{2,3},{3,2},{4,5},{5,4},{6,7},{7,6},{8,9},{9,8},{10,11... | collective-permute-start | bytes 1449992 | tf_op jit(solution)/shard_map/ppermute | solution.py:62
  203.5 7.5 %all-to-all-start.5 = ((bf16[64,48,128]{2,1,0:T(8,128)(2,1)}), bf16[64,48,128]{2,1,0:T(8,128)(2,1)S(1)}, u32[]{:S(2)}, u32[]{:S(2)}) async-start(bf16[64,48,128]{2,1,0:T(8,128)(2,1)} %add_convert_fusion.2), calls=%async_computation.5 | async-start | bytes 1572864 | tf_op jit(solution)/shard_map/all_to_all | solution.py:54
  211.1 2.9 %collective-permute-done.18 = bf16[1888,128]{1,0:T(8,128)(2,1)S(1)} collective-permute-done((bf16[1888,128]{1,0:T(8,128)(2,1)S(1)}, bf16[1888,128]{1,0:T(8,128)(2,1)S(1)}, u32[]{:S(2)}, u32[]{:S(2)}) %collective-permute-start.18) | collective-permute-done | bytes 483360 | tf_op jit(solution)/shard_map/ppermute | solution.py:62
  223.1 3.6 %collective-permute-done.23 = bf16[352,128]{1,0:T(8,128)(2,1)S(1)} collective-permute-done((bf16[352,128]{1,0:T(8,128)(2,1)S(1)}, bf16[352,128]{1,0:T(8,128)(2,1)S(1)}, u32[]{:S(2)}, u32[]{:S(2)}) %collective-permute-start.23) | collective-permute-done | bytes 90144 | tf_op jit(solution)/shard_map/ppermute | solution.py:62
  228.7 3.5 %all-to-all-start.6 = ((bf16[8,384,128]{2,1,0:T(8,128)(2,1)}), bf16[8,384,128]{2,1,0:T(8,128)(2,1)S(1)}, u32[]{:S(2)}, u32[]{:S(2)}) async-start(bf16[8,384,128]{2,1,0:T(8,128)(2,1)} %broadcast_in_dim.46), calls=%async_computation.6 | async-start | bytes 1572864 | tf_op jit(solution)/shard_map/all_to_all | solution.py:54
  242.6 6.0 %collective-permute-done.21 = bf16[256,1024]{1,0:T(8,128)(2,1)} collective-permute-done((bf16[256,1024]{1,0:T(8,128)(2,1)S(1)}, bf16[256,1024]{1,0:T(8,128)(2,1)}, u32[]{:S(2)}, u32[]{:S(2)}) %collective-permute-start.21) | collective-permute-done | bytes 524320 | tf_op jit(solution)/shard_map/ppermute | solution.py:66
  260.2 3.5 %last.1 = (f32[128,3072]{1,0:T(8,128)}, f32[128,1024]{1,0:T(8,128)}, f32[384]{0:T(512)}, f32[1,128]{1,0:T(1,128)}, f32[1,128]{1,0:T(1,128)}, /*index=5*/f32[1,128]{1,0:T(1,128)}, f32[1,128]{1,0:T(1,128)}) custom-call(s32[5]{0:T(128)} %stack.35.ids, bf16[8,384,128]{2,1,0:T(8,128)(2,1)} %copy-done.7, bf16[8,384,128]{2,1,0:T(8,128)(2,1)} %collective-permute-done.24.refs_1_), custom_call_target="tpu_custom_call" | custom-call | bytes 1 | tf_op jit(solution)/shard_map/last/pallas_call | solution.py:165
  264.5 4.8 %mlp_grad.1 = (f32[128,5632]{1,0:T(8,128)}, f32[352,1024]{1,0:T(8,128)}) custom-call(s32[5]{0:T(128)} %stack.35.ids, bf16[1120,128]{1,0:T(8,128)(2,1)} %copy-done.15, bf16[1120,128]{1,0:T(8,128)(2,1)} %collective-permute-done.26.refs_1_, bf16[1120,128]{1,0:T(8,128)(2,1)} %collective-permute-done.28.refs_2_, ...), custom_call_target="tpu_custom_call" | custom-call | bytes 1 | tf_op jit(solution)/shard_map/mlp_grad/pallas_call | solution.py:165
  (186 shorter events, 73.4 us)
Async XLA Ops:
  52.4 19.4 %collective-permute-start.3 = (bf16[352,1024]{1,0:T(8,128)(2,1)S(1)}, bf16[352,1024]{1,0:T(8,128)(2,1)S(1)}, u32[]{:S(2)}, u32[]{:S(2)}) collective-permute-start(bf16[352,1024]{1,0:T(8,128)(2,1)S(1)} %copy-done.17), channel_id=1, source_target_pairs={{0,1},{1,0},{2,3},{3,2},{4,5},{5,4},{6,7},{7,6},{8,9},{9,8},{10,11... | collective-permute-start | bytes 2162696 | tf_op jit(solution)/shard_map/ppermute | solution.py:62
  53.5 18.4 %collective-permute-start.1 = (bf16[8,320,128]{2,1,0:T(8,128)(2,1)S(1)}, bf16[8,320,128]{2,1,0:T(8,128)(2,1)}, u32[]{:S(2)}, u32[]{:S(2)}) collective-permute-start(bf16[8,320,128]{2,1,0:T(8,128)(2,1)S(1)} %slice.74.refs_0_), channel_id=1, source_target_pairs={{0,16},{16,32},{32,48},{48,0},{1,17},{17,33},{33,49},{49,1},{2,18}... | collective-permute-start | bytes 1966088 | tf_op jit(solution)/shard_map/ppermute | solution.py:66
  54.8 17.1 %collective-permute-start.2 = (bf16[8,320,128]{2,1,0:T(8,128)(2,1)S(1)}, bf16[8,320,128]{2,1,0:T(8,128)(2,1)}, u32[]{:S(2)}, u32[]{:S(2)}) collective-permute-start(bf16[8,320,128]{2,1,0:T(8,128)(2,1)S(1)} %slice.74.refs_0_), channel_id=1, source_target_pairs={{0,48},{16,0},{32,16},{48,32},{1,49},{17,1},{33,17},{49,33},{2,50}... | collective-permute-start | bytes 1966088 | tf_op jit(solution)/shard_map/ppermute | solution.py:66
  69.4 17.6 %collective-permute-start.4 = (bf16[8,320,128]{2,1,0:T(8,128)(2,1)S(1)}, bf16[8,320,128]{2,1,0:T(8,128)(2,1)}, u32[]{:S(2)}, u32[]{:S(2)}) collective-permute-start(bf16[8,320,128]{2,1,0:T(8,128)(2,1)S(1)} %slice.74.refs_0_), channel_id=1, source_target_pairs={{0,32},{16,48},{32,0},{48,16},{1,33},{17,49},{33,1},{49,17},{2,34}... | collective-permute-start | bytes 1966088 | tf_op jit(solution)/shard_map/ppermute | solution.py:66
  71.2 17.4 %collective-permute-start.5 = (bf16[8,320,128]{2,1,0:T(8,128)(2,1)S(1)}, bf16[8,320,128]{2,1,0:T(8,128)(2,1)}, u32[]{:S(2)}, u32[]{:S(2)}) collective-permute-start(bf16[8,320,128]{2,1,0:T(8,128)(2,1)S(1)} %slice.74.refs_0_), channel_id=1, source_target_pairs={{0,8},{8,0},{1,9},{9,1},{2,10},{10,2},{3,11},{11,3},{4,12},{12,4},... | collective-permute-start | bytes 1966088 | tf_op jit(solution)/shard_map/ppermute | solution.py:62
  71.9 18.6 %collective-permute-start.6 = (bf16[8,320,128]{2,1,0:T(8,128)(2,1)}, bf16[8,320,128]{2,1,0:T(8,128)(2,1)S(1)}, u32[]{:S(2)}, u32[]{:S(2)}) collective-permute-start(bf16[8,320,128]{2,1,0:T(8,128)(2,1)} %collective-permute-done.1.refs_1_), channel_id=1, source_target_pairs={{0,8},{8,0},{1,9},{9,1},{2,10},{10,2},{3,11},{11,3},{4,12},{12,4},... | collective-permute-start | bytes 1966088 | tf_op jit(solution)/shard_map/ppermute | solution.py:62
  72.8 32.7 %all-to-all-start.1 = ((bf16[8,512,128]{2,1,0:T(8,128)(2,1)}), bf16[8,512,128]{2,1,0:T(8,128)(2,1)S(1)}, u32[]{:S(2)}, u32[]{:S(2)}) async-start(bf16[8,512,128]{2,1,0:T(8,128)(2,1)} %get-tuple-element.78), calls=%async_computation.1 | async-start | bytes 2097152 | tf_op jit(solution)/shard_map/all_to_all | solution.py:54
  76.8 20.0 %collective-permute-start.8 = (bf16[8,320,128]{2,1,0:T(8,128)(2,1)}, bf16[8,320,128]{2,1,0:T(8,128)(2,1)}, u32[]{:S(2)}, u32[]{:S(2)}) collective-permute-start(bf16[8,320,128]{2,1,0:T(8,128)(2,1)} %collective-permute-done.2.refs_3_), channel_id=1, source_target_pairs={{0,8},{8,0},{1,9},{9,1},{2,10},{10,2},{3,11},{11,3},{4,12},{12,4},... | collective-permute-start | bytes 1966088 | tf_op jit(solution)/shard_map/ppermute | solution.py:62
  135.0 18.8 %all-to-all-start.2 = ((bf16[4,128,1024]{2,1,0:T(8,128)(2,1)}), bf16[4,128,1024]{2,1,0:T(8,128)(2,1)S(1)}, u32[]{:S(2)}, u32[]{:S(2)}) async-start(bf16[4,128,1024]{2,1,0:T(8,128)(2,1)} %get-tuple-element.85), calls=%async_computation.2 | async-start | bytes 2097152 | tf_op jit(solution)/shard_map/all_to_all | solution.py:54
  144.6 18.3 %collective-permute-start.13 = (bf16[2240,128]{1,0:T(8,128)(2,1)}, bf16[2240,128]{1,0:T(8,128)(2,1)}, u32[]{:S(2)}, u32[]{:S(2)}) collective-permute-start(bf16[2240,128]{1,0:T(8,128)(2,1)} %get-tuple-element.127), channel_id=1, source_target_pairs={{0,48},{16,0},{32,16},{48,32},{1,49},{17,1},{33,17},{49,33},{2,50}... | collective-permute-start | bytes 1720328 | tf_op jit(solution)/shard_map/ppermute | solution.py:66
  146.3 16.6 %collective-permute-start.14 = (bf16[2240,128]{1,0:T(8,128)(2,1)S(1)}, bf16[2240,128]{1,0:T(8,128)(2,1)}, u32[]{:S(2)}, u32[]{:S(2)}) collective-permute-start(bf16[2240,128]{1,0:T(8,128)(2,1)S(1)} %get-tuple-element.129), channel_id=1, source_target_pairs={{0,32},{16,48},{32,0},{48,16},{1,33},{17,49},{33,1},{49,17},{2,34}... | collective-permute-start | bytes 1720328 | tf_op jit(solution)/shard_map/ppermute | solution.py:66
  146.7 28.4 %collective-permute-start.15 = (bf16[2240,128]{1,0:T(8,128)(2,1)S(1)}, bf16[2240,128]{1,0:T(8,128)(2,1)}, u32[]{:S(2)}, u32[]{:S(2)}) collective-permute-start(bf16[2240,128]{1,0:T(8,128)(2,1)S(1)} %get-tuple-element.128), channel_id=1, source_target_pairs={{0,16},{16,32},{32,48},{48,0},{1,17},{17,33},{33,49},{49,1},{2,18}... | collective-permute-start | bytes 1720328 | tf_op jit(solution)/shard_map/ppermute | solution.py:66
  147.2 47.2 %collective-permute-start.16 = (bf16[384,1024]{1,0:T(8,128)(2,1)S(1)}, bf16[384,1024]{1,0:T(8,128)(2,1)}, u32[]{:S(2)}, u32[]{:S(2)}) collective-permute-start(bf16[384,1024]{1,0:T(8,128)(2,1)S(1)} %copy-done.9), channel_id=1, source_target_pairs={{0,1},{1,0},{2,3},{3,2},{4,5},{5,4},{6,7},{7,6},{8,9},{9,8},{10,11... | collective-permute-start | bytes 2359304 | tf_op jit(solution)/shard_map/ppermute | solution.py:62
  159.4 18.5 %all-to-all-start.3 = ((bf16[8,384,128]{2,1,0:T(8,128)(2,1)}), bf16[8,384,128]{2,1,0:T(8,128)(2,1)S(1)}, u32[]{:S(2)}, u32[]{:S(2)}) async-start(bf16[8,384,128]{2,1,0:T(8,128)(2,1)} %get-tuple-element.86), calls=%async_computation.3 | async-start | bytes 1572864 | tf_op jit(solution)/shard_map/all_to_all | solution.py:54
  177.9 16.5 %all-to-all-start.4 = ((bf16[16,96,128]{2,1,0:T(8,128)(2,1)}), bf16[16,96,128]{2,1,0:T(8,128)(2,1)S(1)}, u32[]{:S(2)}, u32[]{:S(2)}) async-start(bf16[16,96,128]{2,1,0:T(8,128)(2,1)} %bitcast.30), calls=%async_computation.4 | async-start | bytes 786432 | tf_op jit(solution)/shard_map/all_to_all | solution.py:54
  203.2 23.5 %collective-permute-start.22 = (bf16[384,128]{1,0:T(8,128)(2,1)S(1)}, bf16[384,128]{1,0:T(8,128)(2,1)}, u32[]{:S(2)}, u32[]{:S(2)}) collective-permute-start(bf16[384,128]{1,0:T(8,128)(2,1)S(1)} %bitcast.117), channel_id=1, source_target_pairs={{0,64},{64,0},{1,65},{65,1},{2,66},{66,2},{3,67},{67,3},{4,68},{68... | collective-permute-start | bytes 294920 | tf_op jit(solution)/shard_map/ppermute | solution.py:62
  203.5 24.1 %all-to-all-start.5 = ((bf16[64,48,128]{2,1,0:T(8,128)(2,1)}), bf16[64,48,128]{2,1,0:T(8,128)(2,1)S(1)}, u32[]{:S(2)}, u32[]{:S(2)}) async-start(bf16[64,48,128]{2,1,0:T(8,128)(2,1)} %add_convert_fusion.2), calls=%async_computation.5 | async-start | bytes 1572864 | tf_op jit(solution)/shard_map/all_to_all | solution.py:54
  219.1 19.5 %collective-permute-start.19 = (bf16[256,1024]{1,0:T(8,128)(2,1)}, bf16[256,1024]{1,0:T(8,128)(2,1)}, u32[]{:S(2)}, u32[]{:S(2)}) collective-permute-start(bf16[256,1024]{1,0:T(8,128)(2,1)} %pad_maximum_fusion.1), channel_id=1, source_target_pairs={{0,6},{2,0},{4,2},{6,4},{1,7},{3,1},{5,3},{7,5},{8,14},{10,8},{12,... | collective-permute-start | bytes 1572872 | tf_op jit(solution)/shard_map/ppermute | solution.py:66
  222.3 17.5 %collective-permute-start.20 = (bf16[256,1024]{1,0:T(8,128)(2,1)}, bf16[256,1024]{1,0:T(8,128)(2,1)}, u32[]{:S(2)}, u32[]{:S(2)}) collective-permute-start(bf16[256,1024]{1,0:T(8,128)(2,1)} %pad_maximum_fusion.2), channel_id=1, source_target_pairs={{0,4},{2,6},{4,0},{6,2},{1,5},{3,7},{5,1},{7,3},{8,12},{10,14},{12... | collective-permute-start | bytes 1572872 | tf_op jit(solution)/shard_map/ppermute | solution.py:66
  228.7 19.8 %all-to-all-start.6 = ((bf16[8,384,128]{2,1,0:T(8,128)(2,1)}), bf16[8,384,128]{2,1,0:T(8,128)(2,1)S(1)}, u32[]{:S(2)}, u32[]{:S(2)}) async-start(bf16[8,384,128]{2,1,0:T(8,128)(2,1)} %broadcast_in_dim.46), calls=%async_computation.6 | async-start | bytes 1572864 | tf_op jit(solution)/shard_map/all_to_all | solution.py:54
  234.8 17.5 %collective-permute-start.26 = (bf16[1120,128]{1,0:T(8,128)(2,1)S(1)}, bf16[1120,128]{1,0:T(8,128)(2,1)}, u32[]{:S(2)}, u32[]{:S(2)}) collective-permute-start(bf16[1120,128]{1,0:T(8,128)(2,1)S(1)} %pad_maximum_fusion.5.refs_0_), channel_id=1, source_target_pairs={{0,16},{16,32},{32,48},{48,0},{1,17},{17,33},{33,49},{49,1},{2,18}... | collective-permute-start | bytes 860168 | tf_op jit(solution)/shard_map/ppermute | solution.py:66
  236.2 19.1 %collective-permute-start.28 = (bf16[1120,128]{1,0:T(8,128)(2,1)S(1)}, bf16[1120,128]{1,0:T(8,128)(2,1)}, u32[]{:S(2)}, u32[]{:S(2)}) collective-permute-start(bf16[1120,128]{1,0:T(8,128)(2,1)S(1)} %pad_maximum_fusion.5.refs_0_), channel_id=1, source_target_pairs={{0,32},{16,48},{32,0},{48,16},{1,33},{17,49},{33,1},{49,17},{2,34}... | collective-permute-start | bytes 860168 | tf_op jit(solution)/shard_map/ppermute | solution.py:66
  238.6 19.3 %collective-permute-start.30 = (bf16[1120,128]{1,0:T(8,128)(2,1)S(1)}, bf16[1120,128]{1,0:T(8,128)(2,1)}, u32[]{:S(2)}, u32[]{:S(2)}) collective-permute-start(bf16[1120,128]{1,0:T(8,128)(2,1)S(1)} %pad_maximum_fusion.5.refs_0_), channel_id=1, source_target_pairs={{0,48},{16,0},{32,16},{48,32},{1,49},{17,1},{33,17},{49,33},{2,50}... | collective-permute-start | bytes 860168 | tf_op jit(solution)/shard_map/ppermute | solution.py:66
  239.8 23.9 %collective-permute-start.25 = (bf16[1120,128]{1,0:T(8,128)(2,1)S(1)}, bf16[1120,128]{1,0:T(8,128)(2,1)}, u32[]{:S(2)}, u32[]{:S(2)}) collective-permute-start(bf16[1120,128]{1,0:T(8,128)(2,1)S(1)} %pad_maximum_fusion.5.refs_0_), channel_id=1, source_target_pairs={{0,8},{8,0},{1,9},{9,1},{2,10},{10,2},{3,11},{11,3},{4,12},{12,4},... | collective-permute-start | bytes 860168 | tf_op jit(solution)/shard_map/ppermute | solution.py:62
  (50 other events, 401.3 us)

commit v2 on v1

--- a/solution.py
+++ b/solution.py
@@ -103,25 +103,33 @@
     def __init__(self, copies, buffer):
         self.copies, self.buffer = copies, buffer
 
-    def arrive(self):
-        for copy in self.copies:
-            copy.wait()
-        self.copies = []
+    def arrive(self, piece=None):
+        for i, copy in enumerate(self.copies):
+            if copy is not None and piece in (None, i):
+                copy.wait()
+                self.copies[i] = None
         return self.buffer
 
     def __getitem__(self, index):
-        return self.arrive()[index]
+        first = index[0] if isinstance(index, tuple) else None
+        piece = first if isinstance(first, int) and len(self.copies) > 1 else None
+        return self.arrive(piece)[index]
 
 
 class Result:
-    def __init__(self, copy, buffer):
-        self.copy, self.buffer, self.sent = copy, buffer, False
+    def __init__(self, source, target, sem):
+        self.copy, self.buffer, self.sent = pltpu.make_async_copy(source, target, sem), source, False
+        self.target, self.sem = target, sem
 
     def __setitem__(self, index, value):
         self.buffer[index] = value
 
     def __getitem__(self, index):
         return self.buffer[index]
+
+    def send_rows(self, rows):
+        pltpu.make_async_copy(self.buffer.at[rows], self.target.at[rows], self.sem).start()
+        self.sent = True
 
     def send(self):
         if not self.sent:
@@ -150,9 +158,7 @@
             for copy in copies:
                 copy.start()
             inputs.append(Later(copies, buffers[i]))
-        outputs = [
-            Result(pltpu.make_async_copy(results[i], targets[i], out_sems.at[i]), results[i]) for i in range(outs)
-        ]
+        outputs = [Result(results[i], targets[i], out_sems.at[i]) for i in range(outs)]
         kernel(ids, *inputs, *outputs, *mine)
         for value in inputs:
             value.arrive()
@@ -186,14 +192,14 @@
     return jnp.concatenate([a * cos - sign * (b * sin), b * cos + sign * (a * sin), value[16:]], axis=0)
 
 
-def qkv_weights(c, packet, other, w_rows, w_out):
+def qkv_weights(c, cols, other, w_rows, w_out):
     mine = pl.multiple_of(c * 64, 64)
     theirs = pl.multiple_of((1 - c) * 64, 64)
     for src in range(8):
         for kind in range(3):
             lanes = slice(kind * 128, kind * 128 + 128)
-            at = QKV_AT + kind * 64
-            w_rows[pl.ds(src * 128 + mine, 64), lanes] = packet[0, src, at : at + 64, :]
+            at = kind * 64
+            w_rows[pl.ds(src * 128 + mine, 64), lanes] = cols[0, src, at : at + 64, :]
             w_rows[pl.ds(src * 128 + theirs, 64), lanes] = other[src, kind * 64 : kind * 64 + 64, :]
     for kind in range(3):
         for src in range(8):
@@ -204,16 +210,17 @@
 
 def normed_kernel(ids, packet, xhat_out):
     for block in range(8):
-        x = jnp.concatenate([packet[0, block, cb * 128 : cb * 128 + 128, :].astype(F32) for cb in range(8)], axis=1)
+        x = jnp.concatenate([packet[block, cb * 128 : cb * 128 + 128, :].astype(F32) for cb in range(8)], axis=1)
         xhat_out[block * 128 : block * 128 + 128, :] = normalize(x)[0].astype(BF16)
-
-
-def attend_kernel(ids, packet, other, cos_ref, sin_ref, qkv_out, attended, lse_out, w_out, w_rows):
+        xhat_out.send_rows(slice(block * 128, block * 128 + 128))
+
+
+def attend_kernel(ids, cols, other, packet, cos_ref, sin_ref, qkv_out, attended, lse_out, w_out, w_rows):
     c = ids[ID_C]
     s = ids[ID_Z] * 2 + ids[ID_XH]
-    qkv_weights(c, packet, other, w_rows, w_out)
+    qkv_weights(c, cols, other, w_rows, w_out)
     w_out.send()
-    vec = [packet[0, src, VEC_AT : VEC_AT + 16, :].astype(F32) for src in range(8)]
+    vec = [packet[src, VEC_AT : VEC_AT + 16, :].astype(F32) for src in range(8)]
     gain = jnp.concatenate([v[0:1] for v in vec], axis=1)
     bias = jnp.concatenate([v[1:2] for v in vec], axis=1)
     row = lax.broadcasted_iota(jnp.int32, (16, 128), 0)
@@ -231,7 +238,7 @@
         x = jnp.concatenate(
             [
                 jnp.concatenate(
-                    [packet[0, 2 * block + i, cb * 128 : cb * 128 + 128, :].astype(F32) for cb in range(8)], axis=1
+                    [packet[2 * block + i, cb * 128 : cb * 128 + 128, :].astype(F32) for cb in range(8)], axis=1
                 )
                 for i in range(2)
             ],
@@ -279,19 +286,18 @@
 
 def weights_kernel(ids, p0, p1, p2, p3, p4, p5, p6, p7, gate_w, up_w, out_w):
     y, c = ids[ID_Y], ids[ID_C]
-    for k, refs in enumerate(((p0, p4), (p1, p5), (p2, p6), (p3, p7))):
-        at = pl.multiple_of(lax.rem(y - k + 4, 4) * 32, 32)
-        for core, ref in enumerate(refs):
-            half = c if core == 0 else 1 - c
-            for src in range(8):
-                rows = pl.ds(src * 128 + at, 32)
-                for cb in range(3):
-                    lanes = slice(core * PAD + cb * 128, core * PAD + cb * 128 + 128)
-                    gate_w[rows, lanes] = ref[src, cb * 32 : cb * 32 + 32, :]
-                    up_w[rows, lanes] = ref[src, 96 + cb * 32 : 96 + cb * 32 + 32, :]
-                for cb in range(4):
-                    lanes = pl.ds(pl.multiple_of(half * 512 + cb * 128, 128), 128)
-                    out_w[rows, lanes] = ref[src, 192 + cb * 32 : 192 + cb * 32 + 32, :]
+    for target, first, tiles in ((out_w, 192, 4), (gate_w, 0, 3), (up_w, 96, 3)):
+        for k, refs in enumerate(((p0, p4), (p1, p5), (p2, p6), (p3, p7))):
+            at = pl.multiple_of(lax.rem(y - k + 4, 4) * 32, 32)
+            for core, ref in enumerate(refs):
+                half = c if core == 0 else 1 - c
+                start = half * 512 if tiles == 4 else core * PAD
+                for src in range(8):
+                    for cb in range(tiles):
+                        lanes = pl.ds(pl.multiple_of(start + cb * 128, 128), 128)
+                        rows = slice(first + cb * 32, first + cb * 32 + 32)
+                        target[pl.ds(src * 128 + at, 32), lanes] = ref[src, rows, :]
+        target.send()
 
 
 def assemble_down(ids, own, other, down_w):
@@ -310,6 +316,7 @@
     ids, out_w, att, x_ref, gate_w, up_w, gain_ref, bias_ref, dy0, dy1, dy2, dy3, down_own, down_other, mixed_own, att_out, small, ds, keep, send, out0, out1, out2, out3, down_w, second_out, hidden_out, dgate_out, dup_out, held
 ):
     z = ids[ID_Z]
+    x_ref.arrive()
     gain = gain_ref[...]
     bias = bias_ref[...]
     gain_sum = jnp.zeros((1, D), F32)
@@ -373,6 +380,8 @@
                         target[place(to_y), at : at + 16, :] = part[
                             i * 16 : i * 16 + 16, base + cb * 128 : base + cb * 128 + 128
                         ]
+    for target in (send, keep):
+        target.send_rows((slice(None), slice(0, 1536)))
     hidden_t = hidden_out[...].T
     held[...] = dot(hidden_t, cotangent((dy0, dy1, dy2, dy3))).astype(BF16)
     for target, half in ((keep, c), (send, 1 - c)):
@@ -382,8 +391,8 @@
                 for cb in range(4):
                     lanes = pl.ds(pl.multiple_of(half * 512 + cb * 128, 128), 128)
                     target[place(cb), rows, :] = held[base + to_xl * 176 : base + to_xl * 176 + 176, lanes]
-    send.send()
-    keep.send()
+    for target in (send, keep):
+        target.send_rows((slice(None), slice(1536, 2240)))
     for pair in range(2):
         part = dot(hidden_out[pair * 256 : pair * 256 + 256, :], down_w[...]).astype(BF16)
         ((out0, out1), (out2, out3))[pair][0][...] = part[:128]
@@ -518,7 +527,7 @@
                     a, b = wide(mine[k], i, z, which), wide(other[k], i, z, which)
                     parts += [jnp.where(zero, a, b), jnp.where(zero, b, a)]
                 gate_up[rows, which * FF : which * FF + FF] = jnp.concatenate(parts, axis=1)
-    gate_up.send()
+            gate_up.send_rows(rows)
     for refs, half in ((mine, c), (other, 1 - c)):
         for k in range(4):
             lanes = pl.ds(pl.multiple_of(half * 512 + place(k, 0)[1] * 128, 128), 128)
@@ -607,12 +616,13 @@
     piece = packet[:, GU_AT:]
     before, after = turn(piece, "y", 1), turn(piece, "y", 3)
     qkv_other = swap(packet[:, QKV_AT:GU_AT], "c")
-    head_of = lambda array: Part(array, 1, (8, GU_AT, 128), lambda ref, ids: [ref.at[:, 0:GU_AT]])
+    cols = Part(packet, 1, (8, GU_AT - QKV_AT, 128), lambda ref, ids: [ref.at[:, QKV_AT:GU_AT]])
+    tokens = Part(packet, 8, (QKV_AT, 128), lambda ref, ids: [ref.at[i, 0:QKV_AT] for i in range(8)])
     qkv_t, att_blocks, lse, w_t = call(
         attend_kernel,
         "attend_forward",
         (shape(384, SEQ), shape(8, 512, 128), shape(8, SEQ, dtype=F32), shape(384, D)),
-        (ids, head_of(packet), qkv_other, cos, sin),
+        (ids, cols, qkv_other, tokens, cos, sin),
         scratch=[pltpu.VMEM((D, 384), BF16)],
     )
     att_blocks, packet_late, dy_now, far = tie(att_blocks, packet, dy_own, piece)
@@ -624,7 +634,7 @@
         normed_kernel,
         "normed_input",
         (shape(SEQ, D),),
-        (ids, Part(packet_late, 1, (8, D, 128), lambda ref, ids: [ref.at[:, 0:D]])),
+        (ids, Part(packet_late, 8, (D, 128), lambda ref, ids: [ref.at[i, 0:D] for i in range(8)])),
     )
     pieces += [swap(p, "c") for p in pieces]
     gate_w, up_w, out_w = call(

time: 274 us -> 273 us (level)
  no operation moved by 1% of the time
where the time goes in v2:
time: 273 us; the launch traced here: 269 us
  Pallas kernels  71.5 us (26%)
  starting transfers between devices  69 us (25%)
  waiting for transfers between devices  47.9 us (18%)
  blocking collectives  47.2 us (17%)
  other arithmetic  16.5 us (6%)
  local copies, waits for them, and re-layouts  12.9 us (5%)
    pallas_call x8, Pallas kernels, call(): pl.pallas_call(body, out_shape=out_shape, in_specs=[pl.BlockSpec(memory_s...  71.5 us
    all_to_all x1, blocking collectives, exchange(): return lax.all_to_all(value, axes, 0, 0, tiled=True)  47.2 us
    ppermute x15, waiting for transfers between devices, turn(): return lax.ppermute(value, axis, [(i, (i + step) % 4) for i in range(4)])  32.1 us
    all_to_all x6, starting transfers between devices, exchange(): return lax.all_to_all(value, axes, 0, 0, tiled=True)  26.7 us
    ppermute x17, starting transfers between devices, swap(): return lax.ppermute(value, axis, [(0, 1), (1, 0)])  23.1 us
    ppermute x15, starting transfers between devices, turn(): return lax.ppermute(value, axis, [(i, (i + step) % 4) for i in range(4)])  19.2 us
    ppermute x17, waiting for transfers between devices, swap(): return lax.ppermute(value, axis, [(0, 1), (1, 0)])  10.4 us
    unnamed x73, local copies, waits for them, and re-layouts  5.68 us
  transfers between devices with their start and end apart: 38, of which 11 were waited for; matrix products, arithmetic and copies ran while one was open for 8% of the time, Pallas kernels for 15%

profile of v2, /device:TPU:1, one launch (start us, length us, event | category | flops | bytes accessed | tf_op | source)
XLA Modules:
  0.0 269.3 jit_solution(3969554539418673632)
XLA Ops:
  5.2 47.2 %all_to_all.35.refs_0_.refs_2_ = bf16[8,1552,128]{2,1,0:T(8,128)(2,1)S(1)} all-to-all(bf16[8,1552,128]{2,1,0:T(8,128)(2,1)S(1)} %pad_maximum_fusion), channel_id=1, replica_groups=mesh['xl'=2,'y'=4,'c'=2,'z'=4,'xh'=2] {'z','xh'}, dimensions={0} | all-to-all | bytes 6356992 | tf_op jit(solution)/shard_map/all_to_all | solution.py:54
  56.4 2.9 %collective-permute-start = (bf16[8,192,128]{2,1,0:T(8,128)(2,1)S(1)}, bf16[8,192,128]{2,1,0:T(8,128)(2,1)}, u32[]{:S(2)}, u32[]{:S(2)}) collective-permute-start(bf16[8,192,128]{2,1,0:T(8,128)(2,1)S(1)} %slice.75), channel_id=1, source_target_pairs={{0,8},{8,0},{1,9},{9,1},{2,10},{10,2},{3,11},{11,3},{4,12},{12,4},... | collective-permute-start | bytes 1179656 | tf_op jit(solution)/shard_map/ppermute | solution.py:62
  60.7 8.7 %attend_forward.1 = (bf16[384,1024]{1,0:T(8,128)(2,1)}, bf16[8,512,128]{2,1,0:T(8,128)(2,1)}, f32[8,1024]{1,0:T(8,128)}, bf16[384,1024]{1,0:T(8,128)(2,1)}) custom-call(s32[5]{0:T(128)} %stack.35.ids, bf16[8,1552,128]{2,1,0:T(8,128)(2,1)} %copy-done.2, bf16[8,192,128]{2,1,0:T(8,128)(2,1)} %collective-permute-done.refs_1_, bf16[8,1552,128]{2,1,0:T(8,128)(2,1)} %copy-done.2, ...), custom_call_target="tpu_custom_call" | custom-call | bytes 1 | tf_op jit(solution)/shard_map/attend_forward/pallas_call | solution.py:171
  72.7 4.1 %all-to-all-start.1 = ((bf16[8,512,128]{2,1,0:T(8,128)(2,1)}), bf16[8,512,128]{2,1,0:T(8,128)(2,1)S(1)}, u32[]{:S(2)}, u32[]{:S(2)}) async-start(bf16[8,512,128]{2,1,0:T(8,128)(2,1)} %get-tuple-element.78), calls=%async_computation.1 | async-start | bytes 2097152 | tf_op jit(solution)/shard_map/all_to_all | solution.py:54
  77.5 9.5 %collective-permute-done.4.refs_2_ = bf16[8,320,128]{2,1,0:T(8,128)(2,1)} collective-permute-done((bf16[8,320,128]{2,1,0:T(8,128)(2,1)S(1)}, bf16[8,320,128]{2,1,0:T(8,128)(2,1)}, u32[]{:S(2)}, u32[]{:S(2)}) %collective-permute-start.4) | collective-permute-done | bytes 655392 | tf_op jit(solution)/shard_map/ppermute | solution.py:66
  92.1 4.3 %normed_input.1.refs_5_ = bf16[1024,1024]{1,0:T(8,128)(2,1)} custom-call(s32[5]{0:T(128)} %stack.35.ids, bf16[8,1552,128]{2,1,0:T(8,128)(2,1)} %copy-done.2), custom_call_target="tpu_custom_call" | custom-call | bytes 1 | tf_op jit(solution)/shard_map/normed_input/pallas_call | solution.py:171
  96.5 6.1 %weights.1 = (bf16[1024,768]{1,0:T(8,128)(2,1)}, bf16[1024,768]{1,0:T(8,128)(2,1)}, bf16[1024,1024]{1,0:T(8,128)(2,1)}) custom-call(s32[5]{0:T(128)} %stack.35.ids, bf16[8,320,128]{2,1,0:T(8,128)(2,1)} %copy-done.11, bf16[8,320,128]{2,1,0:T(8,128)(2,1)} %collective-permute-done.1.refs_1_, bf16[8,320,128]{2,1,0:T(8,128)(2,1)} %collective-permute-done.4.refs_2_, ...), custom_call_target="tpu_custom_call" | custom-call | bytes 1 | tf_op jit(solution)/shard_map/weights/pallas_call | solution.py:171
  106.5 28.0 %mlp.1 = (f32[128,1024]{1,0:T(8,128)}, bf16[512,1024]{1,0:T(8,128)(2,1)}, f32[8,1024]{1,0:T(8,128)}, bf16[4,128,1024]{2,1,0:T(8,128)(2,1)}, bf16[4,2240,128]{2,1...) custom-call(s32[5]{0:T(128)} %stack.35.ids, ...), custom_call_target="tpu_custom_call" | custom-call | bytes 1 | tf_op jit(solution)/shard_map/mlp/pallas_call | solution.py:171
  135.2 3.5 %all-to-all-start.2 = ((bf16[4,128,1024]{2,1,0:T(8,128)(2,1)}), bf16[4,128,1024]{2,1,0:T(8,128)(2,1)S(1)}, u32[]{:S(2)}, u32[]{:S(2)}) async-start(bf16[4,128,1024]{2,1,0:T(8,128)(2,1)} %get-tuple-element.85), calls=%async_computation.2 | async-start | bytes 2097152 | tf_op jit(solution)/shard_map/all_to_all | solution.py:54
  139.6 2.9 %add_convert_fusion = bf16[4,2240,128]{2,1,0:T(8,128)(2,1)S(1)} fusion(bf16[4,2240,128]{2,1,0:T(8,128)(2,1)} %collective-permute-done.12, bf16[4,2240,128]{2,1,0:T(8,128)(2,1)} %get-tuple-element.96), kind=kLoop, calls=%fused_computation | loop fusion | flops 4587520 | bytes 6881280 | tf_op jit(solution)/shard_map/convert_element_type | solution.py:687
  148.7 5.3 %all-to-all-done.2.refs_0_ = bf16[4,128,1024]{2,1,0:T(8,128)(2,1)S(1)} async-done(((bf16[4,128,1024]{2,1,0:T(8,128)(2,1)}), bf16[4,128,1024]{2,1,0:T(8,128)(2,1)S(1)}, u32[]{:S(2)}, u32[]{:S(2)}) %all-to-all-start.2) | async-done | bytes 1048608 | tf_op jit(solution)/shard_map/all_to_all | solution.py:54
  155.0 4.6 %norm_backward.1 = (f32[128,1024]{1,0:T(8,128)}, bf16[8,384,128]{2,1,0:T(8,128)(2,1)}) custom-call(s32[5]{0:T(128)} %stack.35.ids, bf16[4,128,1024]{2,1,0:T(8,128)(2,1)} %copy-done.5, bf16[128,1024]{1,0:T(8,128)(2,1)} %bitcast.110, f32[128,1024]{1,0:T(8,128)} %get-tuple-element.83.refs_2_, f32[1,1024]{1,0:T(1,128)} %get-tuple-element.143.refs_5_.refs_3_, ...), custom_call_target="tpu_custom_call" | custom-call | bytes 1 | tf_op jit(solution)/shard_map/norm_backward/pallas_call | solution.py:171
  159.6 3.6 %all-to-all-start.3 = ((bf16[8,384,128]{2,1,0:T(8,128)(2,1)}), bf16[8,384,128]{2,1,0:T(8,128)(2,1)S(1)}, u32[]{:S(2)}, u32[]{:S(2)}) async-start(bf16[8,384,128]{2,1,0:T(8,128)(2,1)} %get-tuple-element.86), calls=%async_computation.3 | async-start | bytes 1572864 | tf_op jit(solution)/shard_map/all_to_all | solution.py:54
  163.2 12.2 %collective-permute-done.15 = bf16[2240,128]{1,0:T(8,128)(2,1)} collective-permute-done((bf16[2240,128]{1,0:T(8,128)(2,1)S(1)}, bf16[2240,128]{1,0:T(8,128)(2,1)}, u32[]{:S(2)}, u32[]{:S(2)}) %collective-permute-start.15) | collective-permute-done | bytes 573472 | tf_op jit(solution)/shard_map/ppermute | solution.py:66
  178.2 4.5 %all-to-all-start.4 = ((bf16[16,96,128]{2,1,0:T(8,128)(2,1)}), bf16[16,96,128]{2,1,0:T(8,128)(2,1)S(1)}, u32[]{:S(2)}, u32[]{:S(2)}) async-start(bf16[16,96,128]{2,1,0:T(8,128)(2,1)} %bitcast.30), calls=%async_computation.4 | async-start | bytes 786432 | tf_op jit(solution)/shard_map/all_to_all | solution.py:54
  182.7 12.0 %attend_backward.1 = (bf16[64,48,128]{2,1,0:T(8,128)(2,1)}, bf16[64,48,128]{2,1,0:T(8,128)(2,1)}, bf16[512,384]{1,0:T(8,128)(2,1)}, bf16[1536,128]{1,0:T(8,128)(2,1)}) custom-call(s32[5]{0:T(128)} %stack.35.ids, bf16[8,384,128]{2,1,0:T(8,128)(2,1)} %copy-done.8, bf16[384,1024]{1,0:T(8,128)(2,1)} %get-tuple-element.87.refs_1_, ...), custom_call_target="tpu_custom_call" | custom-call | bytes 1 | tf_op jit(solution)/shard_map/attend_backward/pallas_call | solution.py:171
  200.0 3.2 %collective-permute-start.18 = (bf16[1888,128]{1,0:T(8,128)(2,1)S(1)}, bf16[1888,128]{1,0:T(8,128)(2,1)S(1)}, u32[]{:S(2)}, u32[]{:S(2)}) collective-permute-start(bf16[1888,128]{1,0:T(8,128)(2,1)S(1)} %pad_maximum_fusion.4), channel_id=1, source_target_pairs={{0,1},{1,0},{2,3},{3,2},{4,5},{5,4},{6,7},{7,6},{8,9},{9,8},{10,11... | collective-permute-start | bytes 1449992 | tf_op jit(solution)/shard_map/ppermute | solution.py:62
  203.8 7.5 %all-to-all-start.5 = ((bf16[64,48,128]{2,1,0:T(8,128)(2,1)}), bf16[64,48,128]{2,1,0:T(8,128)(2,1)S(1)}, u32[]{:S(2)}, u32[]{:S(2)}) async-start(bf16[64,48,128]{2,1,0:T(8,128)(2,1)} %add_convert_fusion.2), calls=%async_computation.5 | async-start | bytes 1572864 | tf_op jit(solution)/shard_map/all_to_all | solution.py:54
  211.3 3.0 %collective-permute-done.18 = bf16[1888,128]{1,0:T(8,128)(2,1)S(1)} collective-permute-done((bf16[1888,128]{1,0:T(8,128)(2,1)S(1)}, bf16[1888,128]{1,0:T(8,128)(2,1)S(1)}, u32[]{:S(2)}, u32[]{:S(2)}) %collective-permute-start.18) | collective-permute-done | bytes 483360 | tf_op jit(solution)/shard_map/ppermute | solution.py:62
  223.3 3.6 %collective-permute-done.23 = bf16[352,128]{1,0:T(8,128)(2,1)S(1)} collective-permute-done((bf16[352,128]{1,0:T(8,128)(2,1)S(1)}, bf16[352,128]{1,0:T(8,128)(2,1)S(1)}, u32[]{:S(2)}, u32[]{:S(2)}) %collective-permute-start.23) | collective-permute-done | bytes 90144 | tf_op jit(solution)/shard_map/ppermute | solution.py:62
  229.0 3.5 %all-to-all-start.6 = ((bf16[8,384,128]{2,1,0:T(8,128)(2,1)}), bf16[8,384,128]{2,1,0:T(8,128)(2,1)S(1)}, u32[]{:S(2)}, u32[]{:S(2)}) async-start(bf16[8,384,128]{2,1,0:T(8,128)(2,1)} %broadcast_in_dim.46), calls=%async_computation.6 | async-start | bytes 1572864 | tf_op jit(solution)/shard_map/all_to_all | solution.py:54
  242.8 6.0 %collective-permute-done.21 = bf16[256,1024]{1,0:T(8,128)(2,1)} collective-permute-done((bf16[256,1024]{1,0:T(8,128)(2,1)S(1)}, bf16[256,1024]{1,0:T(8,128)(2,1)}, u32[]{:S(2)}, u32[]{:S(2)}) %collective-permute-start.21) | collective-permute-done | bytes 524320 | tf_op jit(solution)/shard_map/ppermute | solution.py:66
  260.4 3.5 %last.1 = (f32[128,3072]{1,0:T(8,128)}, f32[128,1024]{1,0:T(8,128)}, f32[384]{0:T(512)}, f32[1,128]{1,0:T(1,128)}, f32[1,128]{1,0:T(1,128)}, /*index=5*/f32[1,128]{1,0:T(1,128)}, f32[1,128]{1,0:T(1,128)}) custom-call(s32[5]{0:T(128)} %stack.35.ids, bf16[8,384,128]{2,1,0:T(8,128)(2,1)} %copy-done.7, bf16[8,384,128]{2,1,0:T(8,128)(2,1)} %collective-permute-done.24.refs_1_), custom_call_target="tpu_custom_call" | custom-call | bytes 1 | tf_op jit(solution)/shard_map/last/pallas_call | solution.py:171
  264.8 4.2 %mlp_grad.1 = (f32[128,5632]{1,0:T(8,128)}, f32[352,1024]{1,0:T(8,128)}) custom-call(s32[5]{0:T(128)} %stack.35.ids, bf16[1120,128]{1,0:T(8,128)(2,1)} %copy-done.15, bf16[1120,128]{1,0:T(8,128)(2,1)} %collective-permute-done.26.refs_1_, bf16[1120,128]{1,0:T(8,128)(2,1)} %collective-permute-done.28.refs_2_, ...), custom_call_target="tpu_custom_call" | custom-call | bytes 1 | tf_op jit(solution)/shard_map/mlp_grad/pallas_call | solution.py:171
  (186 shorter events, 73.5 us)
Async XLA Ops:
  52.4 19.4 %collective-permute-start.3 = (bf16[352,1024]{1,0:T(8,128)(2,1)S(1)}, bf16[352,1024]{1,0:T(8,128)(2,1)S(1)}, u32[]{:S(2)}, u32[]{:S(2)}) collective-permute-start(bf16[352,1024]{1,0:T(8,128)(2,1)S(1)} %copy-done.17), channel_id=1, source_target_pairs={{0,1},{1,0},{2,3},{3,2},{4,5},{5,4},{6,7},{7,6},{8,9},{9,8},{10,11... | collective-permute-start | bytes 2162696 | tf_op jit(solution)/shard_map/ppermute | solution.py:62
  53.5 18.4 %collective-permute-start.1 = (bf16[8,320,128]{2,1,0:T(8,128)(2,1)S(1)}, bf16[8,320,128]{2,1,0:T(8,128)(2,1)}, u32[]{:S(2)}, u32[]{:S(2)}) collective-permute-start(bf16[8,320,128]{2,1,0:T(8,128)(2,1)S(1)} %slice.74.refs_0_), channel_id=1, source_target_pairs={{0,16},{16,32},{32,48},{48,0},{1,17},{17,33},{33,49},{49,1},{2,18}... | collective-permute-start | bytes 1966088 | tf_op jit(solution)/shard_map/ppermute | solution.py:66
  54.8 17.0 %collective-permute-start.2 = (bf16[8,320,128]{2,1,0:T(8,128)(2,1)S(1)}, bf16[8,320,128]{2,1,0:T(8,128)(2,1)}, u32[]{:S(2)}, u32[]{:S(2)}) collective-permute-start(bf16[8,320,128]{2,1,0:T(8,128)(2,1)S(1)} %slice.74.refs_0_), channel_id=1, source_target_pairs={{0,48},{16,0},{32,16},{48,32},{1,49},{17,1},{33,17},{49,33},{2,50}... | collective-permute-start | bytes 1966088 | tf_op jit(solution)/shard_map/ppermute | solution.py:66
  69.4 17.6 %collective-permute-start.4 = (bf16[8,320,128]{2,1,0:T(8,128)(2,1)S(1)}, bf16[8,320,128]{2,1,0:T(8,128)(2,1)}, u32[]{:S(2)}, u32[]{:S(2)}) collective-permute-start(bf16[8,320,128]{2,1,0:T(8,128)(2,1)S(1)} %slice.74.refs_0_), channel_id=1, source_target_pairs={{0,32},{16,48},{32,0},{48,16},{1,33},{17,49},{33,1},{49,17},{2,34}... | collective-permute-start | bytes 1966088 | tf_op jit(solution)/shard_map/ppermute | solution.py:66
  71.2 17.4 %collective-permute-start.5 = (bf16[8,320,128]{2,1,0:T(8,128)(2,1)S(1)}, bf16[8,320,128]{2,1,0:T(8,128)(2,1)}, u32[]{:S(2)}, u32[]{:S(2)}) collective-permute-start(bf16[8,320,128]{2,1,0:T(8,128)(2,1)S(1)} %slice.74.refs_0_), channel_id=1, source_target_pairs={{0,8},{8,0},{1,9},{9,1},{2,10},{10,2},{3,11},{11,3},{4,12},{12,4},... | collective-permute-start | bytes 1966088 | tf_op jit(solution)/shard_map/ppermute | solution.py:62
  71.9 18.6 %collective-permute-start.6 = (bf16[8,320,128]{2,1,0:T(8,128)(2,1)}, bf16[8,320,128]{2,1,0:T(8,128)(2,1)S(1)}, u32[]{:S(2)}, u32[]{:S(2)}) collective-permute-start(bf16[8,320,128]{2,1,0:T(8,128)(2,1)} %collective-permute-done.1.refs_1_), channel_id=1, source_target_pairs={{0,8},{8,0},{1,9},{9,1},{2,10},{10,2},{3,11},{11,3},{4,12},{12,4},... | collective-permute-start | bytes 1966088 | tf_op jit(solution)/shard_map/ppermute | solution.py:62
  72.7 32.7 %all-to-all-start.1 = ((bf16[8,512,128]{2,1,0:T(8,128)(2,1)}), bf16[8,512,128]{2,1,0:T(8,128)(2,1)S(1)}, u32[]{:S(2)}, u32[]{:S(2)}) async-start(bf16[8,512,128]{2,1,0:T(8,128)(2,1)} %get-tuple-element.78), calls=%async_computation.1 | async-start | bytes 2097152 | tf_op jit(solution)/shard_map/all_to_all | solution.py:54
  76.8 19.6 %collective-permute-start.8 = (bf16[8,320,128]{2,1,0:T(8,128)(2,1)}, bf16[8,320,128]{2,1,0:T(8,128)(2,1)}, u32[]{:S(2)}, u32[]{:S(2)}) collective-permute-start(bf16[8,320,128]{2,1,0:T(8,128)(2,1)} %collective-permute-done.2.refs_3_), channel_id=1, source_target_pairs={{0,8},{8,0},{1,9},{9,1},{2,10},{10,2},{3,11},{11,3},{4,12},{12,4},... | collective-permute-start | bytes 1966088 | tf_op jit(solution)/shard_map/ppermute | solution.py:62
  135.2 18.8 %all-to-all-start.2 = ((bf16[4,128,1024]{2,1,0:T(8,128)(2,1)}), bf16[4,128,1024]{2,1,0:T(8,128)(2,1)S(1)}, u32[]{:S(2)}, u32[]{:S(2)}) async-start(bf16[4,128,1024]{2,1,0:T(8,128)(2,1)} %get-tuple-element.85), calls=%async_computation.2 | async-start | bytes 2097152 | tf_op jit(solution)/shard_map/all_to_all | solution.py:54
  144.8 18.3 %collective-permute-start.13 = (bf16[2240,128]{1,0:T(8,128)(2,1)}, bf16[2240,128]{1,0:T(8,128)(2,1)}, u32[]{:S(2)}, u32[]{:S(2)}) collective-permute-start(bf16[2240,128]{1,0:T(8,128)(2,1)} %get-tuple-element.127), channel_id=1, source_target_pairs={{0,48},{16,0},{32,16},{48,32},{1,49},{17,1},{33,17},{49,33},{2,50}... | collective-permute-start | bytes 1720328 | tf_op jit(solution)/shard_map/ppermute | solution.py:66
  146.6 16.6 %collective-permute-start.14 = (bf16[2240,128]{1,0:T(8,128)(2,1)S(1)}, bf16[2240,128]{1,0:T(8,128)(2,1)}, u32[]{:S(2)}, u32[]{:S(2)}) collective-permute-start(bf16[2240,128]{1,0:T(8,128)(2,1)S(1)} %get-tuple-element.129), channel_id=1, source_target_pairs={{0,32},{16,48},{32,0},{48,16},{1,33},{17,49},{33,1},{49,17},{2,34}... | collective-permute-start | bytes 1720328 | tf_op jit(solution)/shard_map/ppermute | solution.py:66
  147.0 28.4 %collective-permute-start.15 = (bf16[2240,128]{1,0:T(8,128)(2,1)S(1)}, bf16[2240,128]{1,0:T(8,128)(2,1)}, u32[]{:S(2)}, u32[]{:S(2)}) collective-permute-start(bf16[2240,128]{1,0:T(8,128)(2,1)S(1)} %get-tuple-element.128), channel_id=1, source_target_pairs={{0,16},{16,32},{32,48},{48,0},{1,17},{17,33},{33,49},{49,1},{2,18}... | collective-permute-start | bytes 1720328 | tf_op jit(solution)/shard_map/ppermute | solution.py:66
  147.5 47.2 %collective-permute-start.16 = (bf16[384,1024]{1,0:T(8,128)(2,1)S(1)}, bf16[384,1024]{1,0:T(8,128)(2,1)}, u32[]{:S(2)}, u32[]{:S(2)}) collective-permute-start(bf16[384,1024]{1,0:T(8,128)(2,1)S(1)} %copy-done.9), channel_id=1, source_target_pairs={{0,1},{1,0},{2,3},{3,2},{4,5},{5,4},{6,7},{7,6},{8,9},{9,8},{10,11... | collective-permute-start | bytes 2359304 | tf_op jit(solution)/shard_map/ppermute | solution.py:62
  159.6 18.6 %all-to-all-start.3 = ((bf16[8,384,128]{2,1,0:T(8,128)(2,1)}), bf16[8,384,128]{2,1,0:T(8,128)(2,1)S(1)}, u32[]{:S(2)}, u32[]{:S(2)}) async-start(bf16[8,384,128]{2,1,0:T(8,128)(2,1)} %get-tuple-element.86), calls=%async_computation.3 | async-start | bytes 1572864 | tf_op jit(solution)/shard_map/all_to_all | solution.py:54
  178.2 16.6 %all-to-all-start.4 = ((bf16[16,96,128]{2,1,0:T(8,128)(2,1)}), bf16[16,96,128]{2,1,0:T(8,128)(2,1)S(1)}, u32[]{:S(2)}, u32[]{:S(2)}) async-start(bf16[16,96,128]{2,1,0:T(8,128)(2,1)} %bitcast.30), calls=%async_computation.4 | async-start | bytes 786432 | tf_op jit(solution)/shard_map/all_to_all | solution.py:54
  203.4 23.5 %collective-permute-start.22 = (bf16[384,128]{1,0:T(8,128)(2,1)S(1)}, bf16[384,128]{1,0:T(8,128)(2,1)}, u32[]{:S(2)}, u32[]{:S(2)}) collective-permute-start(bf16[384,128]{1,0:T(8,128)(2,1)S(1)} %bitcast.117), channel_id=1, source_target_pairs={{0,64},{64,0},{1,65},{65,1},{2,66},{66,2},{3,67},{67,3},{4,68},{68... | collective-permute-start | bytes 294920 | tf_op jit(solution)/shard_map/ppermute | solution.py:62
  203.8 24.1 %all-to-all-start.5 = ((bf16[64,48,128]{2,1,0:T(8,128)(2,1)}), bf16[64,48,128]{2,1,0:T(8,128)(2,1)S(1)}, u32[]{:S(2)}, u32[]{:S(2)}) async-start(bf16[64,48,128]{2,1,0:T(8,128)(2,1)} %add_convert_fusion.2), calls=%async_computation.5 | async-start | bytes 1572864 | tf_op jit(solution)/shard_map/all_to_all | solution.py:54
  219.3 19.5 %collective-permute-start.19 = (bf16[256,1024]{1,0:T(8,128)(2,1)}, bf16[256,1024]{1,0:T(8,128)(2,1)}, u32[]{:S(2)}, u32[]{:S(2)}) collective-permute-start(bf16[256,1024]{1,0:T(8,128)(2,1)} %pad_maximum_fusion.1), channel_id=1, source_target_pairs={{0,6},{2,0},{4,2},{6,4},{1,7},{3,1},{5,3},{7,5},{8,14},{10,8},{12,... | collective-permute-start | bytes 1572872 | tf_op jit(solution)/shard_map/ppermute | solution.py:66
  222.6 17.5 %collective-permute-start.20 = (bf16[256,1024]{1,0:T(8,128)(2,1)}, bf16[256,1024]{1,0:T(8,128)(2,1)}, u32[]{:S(2)}, u32[]{:S(2)}) collective-permute-start(bf16[256,1024]{1,0:T(8,128)(2,1)} %pad_maximum_fusion.2), channel_id=1, source_target_pairs={{0,4},{2,6},{4,0},{6,2},{1,5},{3,7},{5,1},{7,3},{8,12},{10,14},{12... | collective-permute-start | bytes 1572872 | tf_op jit(solution)/shard_map/ppermute | solution.py:66
  229.0 19.8 %all-to-all-start.6 = ((bf16[8,384,128]{2,1,0:T(8,128)(2,1)}), bf16[8,384,128]{2,1,0:T(8,128)(2,1)S(1)}, u32[]{:S(2)}, u32[]{:S(2)}) async-start(bf16[8,384,128]{2,1,0:T(8,128)(2,1)} %broadcast_in_dim.46), calls=%async_computation.6 | async-start | bytes 1572864 | tf_op jit(solution)/shard_map/all_to_all | solution.py:54
  235.1 17.5 %collective-permute-start.26 = (bf16[1120,128]{1,0:T(8,128)(2,1)S(1)}, bf16[1120,128]{1,0:T(8,128)(2,1)}, u32[]{:S(2)}, u32[]{:S(2)}) collective-permute-start(bf16[1120,128]{1,0:T(8,128)(2,1)S(1)} %pad_maximum_fusion.5.refs_0_), channel_id=1, source_target_pairs={{0,16},{16,32},{32,48},{48,0},{1,17},{17,33},{33,49},{49,1},{2,18}... | collective-permute-start | bytes 860168 | tf_op jit(solution)/shard_map/ppermute | solution.py:66
  236.5 19.1 %collective-permute-start.28 = (bf16[1120,128]{1,0:T(8,128)(2,1)S(1)}, bf16[1120,128]{1,0:T(8,128)(2,1)}, u32[]{:S(2)}, u32[]{:S(2)}) collective-permute-start(bf16[1120,128]{1,0:T(8,128)(2,1)S(1)} %pad_maximum_fusion.5.refs_0_), channel_id=1, source_target_pairs={{0,32},{16,48},{32,0},{48,16},{1,33},{17,49},{33,1},{49,17},{2,34}... | collective-permute-start | bytes 860168 | tf_op jit(solution)/shard_map/ppermute | solution.py:66
  238.9 19.3 %collective-permute-start.30 = (bf16[1120,128]{1,0:T(8,128)(2,1)S(1)}, bf16[1120,128]{1,0:T(8,128)(2,1)}, u32[]{:S(2)}, u32[]{:S(2)}) collective-permute-start(bf16[1120,128]{1,0:T(8,128)(2,1)S(1)} %pad_maximum_fusion.5.refs_0_), channel_id=1, source_target_pairs={{0,48},{16,0},{32,16},{48,32},{1,49},{17,1},{33,17},{49,33},{2,50}... | collective-permute-start | bytes 860168 | tf_op jit(solution)/shard_map/ppermute | solution.py:66
  240.1 23.9 %collective-permute-start.25 = (bf16[1120,128]{1,0:T(8,128)(2,1)S(1)}, bf16[1120,128]{1,0:T(8,128)(2,1)}, u32[]{:S(2)}, u32[]{:S(2)}) collective-permute-start(bf16[1120,128]{1,0:T(8,128)(2,1)S(1)} %pad_maximum_fusion.5.refs_0_), channel_id=1, source_target_pairs={{0,8},{8,0},{1,9},{9,1},{2,10},{10,2},{3,11},{11,3},{4,12},{12,4},... | collective-permute-start | bytes 860168 | tf_op jit(solution)/shard_map/ppermute | solution.py:62
  (50 other events, 398.4 us)
